TPU v7x, 32 devices: a whole 2x2x4 slice. The times are simulated.
32 devices in a mesh: groups: 2 (over y), vocab: 4 (over z), rows: 2 (over x), teach: 2 (over core).
Axes of the slice: x: 2, y: 2, z: 4, core: 2. Of those that a mesh axis runs over, the one named last changes fastest.
Arguments:
- hidden_rows: bfloat16 [32, 3584], P(('groups', 'vocab')), parts along dimension 0, may hold values from -512 to 512
- mentor_unnormalized: float32 [32, 4864], P(('groups', 'teach'), ('vocab', 'rows')), parts along dimension 0, may hold values from -1000 to 1000
- head_weight: bfloat16 [4864, 3584], P(('vocab', 'rows', 'teach')), may hold values from -2 to 2
- row_mask: int32 [32], P('groups'), parts along dimension 0, may hold values 0 or 1
Outputs:
- divergence: float32 [32], P('groups'), parts along dimension 0
- hidden_grad: bfloat16 [32, 3584], P(('groups', 'vocab', 'rows', 'teach')), parts along dimension 0
- weight_grad: bfloat16 [9728, 3584], P(('groups', 'vocab', 'rows', 'teach')), parts along dimension 0
There are 2 independent parts, one for each index of `groups`. A program takes and returns all parts, laid end to end along the dimension named above; an argument that names none is the same for every part. Nothing has to cross between parts.
All inputs are finite; a program needn't handle non-finite values.
Results may differ from a plain program's by a relative error of at most 0.0051.
Values may be sent and summed in bfloat16 or wider, within the bound.
A program may use at most 64 MiB of HBM per device.

v0:
```python
import jax
import jax.numpy as jnp
from jax import lax
from jax.sharding import PartitionSpec as P

smoothing_divisor = 2.0
objective_scale = 256.0


def body(hidden_rows, mentor_unnormalized, head_weight, row_mask):
    mentor_divided = lax.all_to_all(
        mentor_unnormalized, "teach", split_axis=1, concat_axis=0, tiled=True
    )
    gathered = lax.all_gather(hidden_rows, "vocab", axis=0, tiled=True)
    head_product_matrix = lax.dot_general(
        gathered, head_weight, (((1,), (1,)), ((), ())), preferred_element_type=jnp.float32
    )
    learner_unnormalized = head_product_matrix / smoothing_divisor
    divided_learner_values = mentor_divided / smoothing_divisor
    max_student, max_teacher = lax.pmax(
        (jnp.max(learner_unnormalized, axis=1), jnp.max(divided_learner_values, axis=1)),
        ("vocab", "rows", "teach"),
    )
    weights_t = jnp.exp(divided_learner_values - max_teacher[:, None])
    sum_student, sum_teacher, cross_term = lax.psum(
        (
            jnp.sum(jnp.exp(learner_unnormalized - max_student[:, None]), axis=1),
            jnp.sum(weights_t, axis=1),
            jnp.sum(weights_t * (divided_learner_values - learner_unnormalized), axis=1),
        ),
        ("vocab", "rows", "teach"),
    )
    lse_student = max_student + jnp.log(sum_student)
    lse_teacher = max_teacher + jnp.log(sum_teacher)
    valid_token_count = row_mask.astype(jnp.float32)
    divergence = valid_token_count * (cross_term / sum_teacher - lse_teacher + lse_student)
    mentor_softmax = jnp.exp(divided_learner_values - lse_teacher[:, None])
    learner_softmax = jnp.exp(learner_unnormalized - lse_student[:, None])
    raw_score_derivative = (
        valid_token_count[:, None]
        * (objective_scale * smoothing_divisor)
        * (learner_softmax - mentor_softmax)
    ).astype(jnp.bfloat16)
    weight_grad = lax.dot_general(
        raw_score_derivative, gathered, (((0,), (0,)), ((), ())), preferred_element_type=jnp.float32
    )
    hidden_grad = lax.psum_scatter(
        jnp.dot(raw_score_derivative, head_weight, preferred_element_type=jnp.float32),
        ("vocab", "rows", "teach"),
        scatter_dimension=0,
        tiled=True,
    )
    return (divergence, hidden_grad.astype(jnp.bfloat16), weight_grad.astype(jnp.bfloat16))


def solution(mesh):
    return jax.shard_map(
        body,
        mesh=mesh,
        in_specs=(
            P(("groups", "vocab"), None),
            P(("groups", "teach"), ("vocab", "rows")),
            P(("vocab", "rows", "teach"), None),
            P("groups"),
        ),
        out_specs=(
            P("groups"),
            P(("groups", "vocab", "rows", "teach"), None),
            P(("groups", "vocab", "rows", "teach"), None),
        ),
        check_vma=False,
    )
```

profile of v0, /device:TPU:0, one launch (start us, length us, event | category | flops | bytes accessed | tf_op | source)
XLA Modules:
  0.0 148.9 jit_solution(4370438108467878461)
XLA Ops:
  0.6 0.0 copy-start
  0.6 1.0 all_to_all.10
  1.6 0.6 copy.8
  2.2 3.2 %all-to-all-start = ((f32[8,2,304]{2,0,1:T(8,128)}), f32[8,2,304]{2,0,1:T(8,128)S(1)}, u32[]{:S(2)}, u32[]{:S(2)}) async-start(f32[8,2,304]{2,0,1:T(8,128)} %copy.8), calls=%async_computation | async-start | bytes 49152 | tf_op jit(solution)/shard_map/all_to_all | solution.py:11
  5.5 0.7 convert_multiply_fusion
  6.1 0.7 all-to-all-done
  6.8 0.1 bitcast_reduce_fusion
  6.9 0.1 reduce_max.21
  7.0 15.3 %all-gather = bf16[4,4,3584]{2,1,0:T(4,128)(2,1)S(1)} all-gather(bf16[1,4,3584]{2,1,0:T(4,128)(2,1)} %bitcast.36), channel_id=1, replica_groups=mesh['groups'=2,'vocab'=4,'rows'=2,'teach'=2] {'vocab'}, dimensions={0}, use_global_device_ids=true | all-gather | bytes 143360 | tf_op jit(solution)/shard_map/all_gather | solution.py:14
  22.3 0.0 copy-done
  22.3 0.8 fusion.9
  23.1 30.6 %all-reduce.3 = (f32[16]{0:T(128)S(1)}, f32[16]{0:T(128)S(1)}) all-reduce(f32[16]{0:T(128)S(1)} %get-tuple-element.11, f32[16]{0:T(128)S(1)} %reduce_max.21), channel_id=1, replica_groups=mesh['groups'=2,'vocab'=4,'rows'=2,'teach'=2] {'vocab','rows','teach'}, use_global_device_ids=true, to_apply=%region_7.0 | all-reduce | flops 32 | bytes 256 | tf_op jit(solution)/shard_map/pmax | solution.py:20
  53.8 0.1 sub.51
  53.8 0.2 fusion.8
  54.0 0.1 reduce_sum.31
  54.1 0.2 fusion.2
  54.3 29.5 %all-reduce.2 = (f32[16]{0:T(128)S(1)}, f32[16]{0:T(128)S(1)}) all-reduce(f32[16]{0:T(128)S(1)} %get-tuple-element.4, f32[16]{0:T(128)S(1)} %reduce_sum.31), channel_id=1, replica_groups=mesh['groups'=2,'vocab'=4,'rows'=2,'teach'=2] {'vocab','rows','teach'}, use_global_device_ids=true, to_apply=%region_9.0 | all-reduce | flops 32 | bytes 256 | tf_op jit(solution)/shard_map/psum | solution.py:25
  83.8 0.1 fusion.6
  83.9 0.0 copy-start.1
  83.9 0.0 copy-start.2
  83.9 0.4 fusion.10
  84.4 2.1 %convolution_convert_fusion = bf16[304,3584]{1,0:T(8,128)(2,1)} fusion(bf16[16,304]{1,0:T(8,128)(2,1)S(1)} %fusion.6, bf16[16,3584]{1,0:T(8,128)(2,1)S(1)} %reshape.24), kind=kOutput, calls=%fused_computation | convolution fusion | flops 35954688 | bytes 2303488 | tf_op jit(solution)/shard_map/dot_general | solution.py:44
  86.5 59.9 %all-reduce.5 = (f32[16]{0:T(128)S(1)}, bf16[16,3584]{1,0:T(8,128)(2,1)S(1)}) all-reduce(f32[16]{0:T(128)S(1)} %get-tuple-element.3, f32[16,3584]{1,0:T(8,128)S(1)} %fusion.10), channel_id=1, replica_groups=mesh['groups'=2,'vocab'=4,'rows'=2,'teach'=2] {'vocab','rows','teach'}, use_global_device_ids=true, to_apply=%region_3.0 | all-reduce | flops 57360 | bytes 344192 | tf_op jit(solution)/shard_map/psum | solution.py:25
  146.4 0.0 copy-done.1
  146.4 0.5 add_multiply_fusion
  146.9 0.0 copy-done.2
  146.9 0.7 dynamic-slice
  147.6 1.3 dynamic-slice_convert_fusion
  (2 shorter events, 0.0 us)
Async XLA Ops:
  0.6 21.7 %copy-start = (bf16[304,3584]{1,0:T(8,128)(2,1)S(1)}, bf16[304,3584]{1,0:T(8,128)(2,1)}, u32[]{:S(2)}) copy-start(bf16[304,3584]{1,0:T(8,128)(2,1)} %param.6) | copy-start | bytes 6537220
  2.2 4.6 %all-to-all-start = ((f32[8,2,304]{2,0,1:T(8,128)}), f32[8,2,304]{2,0,1:T(8,128)S(1)}, u32[]{:S(2)}, u32[]{:S(2)}) async-start(f32[8,2,304]{2,0,1:T(8,128)} %copy.8), calls=%async_computation | async-start | bytes 49152 | tf_op jit(solution)/shard_map/all_to_all | solution.py:11
  83.9 62.5 %copy-start.1 = (s32[16]{0:T(128)S(1)}, s32[16]{0:T(128)}, u32[]{:S(2)}) copy-start(s32[16]{0:T(128)} %param.7) | copy-start | bytes 196
  83.9 63.0 %copy-start.2 = (u32[32]{0:T(128)S(1)}, u32[32]{0:T(128)}, u32[]{:S(2)}) copy-start(u32[32]{0:T(128)} %constant.13) | copy-start | bytes 388
where the time goes:
time: 149 us
  blocking collectives  135 us (91%)
  local copies, waits for them, and re-layouts  3.85 us (3%)
  matrix products  3.34 us (2%)
  starting transfers between devices  3.25 us (2%)
  other arithmetic  1.73 us (1%)
    psum x2, blocking collectives, body(): lax.psum((jnp.sum(jnp.exp(learner_unnormalized - max_student[:, None]), a...  89.4 us
    pmax x1, blocking collectives, body(): lax.pmax((jnp.max(learner_unnormalized, axis=1), jnp.max(divided_learner_...  30.6 us
    all_gather x1, blocking collectives, body(): gathered = lax.all_gather(hidden_rows, 'vocab', axis=0, tiled=True)  15.3 us
    all_to_all x1, starting transfers between devices, body(): lax.all_to_all(mentor_unnormalized, 'teach', split_axis=1, concat_axis=0,...  3.25 us
  transfers between devices with their start and end apart: 1, of which 1 were waited for; matrix products, arithmetic and copies ran while one was open for 0% of the time, Pallas kernels for 0%

commit v1 on v0

v1 whole, which is shorter than its diff:
```python
import functools

import jax
import jax.numpy as jnp
from jax import lax
from jax.experimental import pallas as pl
from jax.experimental.pallas import tpu as pltpu
from jax.sharding import PartitionSpec as P

smoothing_divisor = 2.0
objective_scale = 256.0

LANES = 128
PACK = 16
CHUNK = 256


def dot(a, b, contract):
    return lax.dot_general(a, b, ((contract[:1], contract[1:]), ((), ())), preferred_element_type=jnp.float32)


def column_to_row(columns, width):
    rows = columns[0].shape[0]
    lane = lax.broadcasted_iota(jnp.int32, (rows, width), 1)
    row = lax.broadcasted_iota(jnp.int32, (rows, width), 0)
    total = jnp.zeros((rows, width), jnp.float32)
    for place, column in enumerate(columns):
        total = jnp.where(lane == row + place * rows, column, total)
    return jnp.sum(total, axis=0, keepdims=True)


def row_to_column(line, place, rows):
    width = line.shape[1]
    lane = lax.broadcasted_iota(jnp.int32, (rows, width), 1)
    row = lax.broadcasted_iota(jnp.int32, (rows, width), 0)
    return jnp.sum(jnp.where(lane == row + place * rows, line, 0.0), axis=1, keepdims=True)


def main_kernel(
    sizes,
    hid, mentor, w_hbm, mask,
    wg, hg, div,
    w, hsend, hrecv, h, tsend, trecv, ssend, srecv, part, gsend, grecv,
    w_sem, hs_sem, hr_sem, ts_sem, tr_sem, ss_sem, sr_sem, gs_sem, gr_sem,
):
    nz, nx, nc = sizes
    n = nz * nx * nc
    own, depth = hid.shape
    rows = own * nz
    vocab = w.shape[0]
    fold = PACK // own
    span = depth // fold
    chunks = depth // CHUNK
    half = mentor.shape[0]
    unroll = n <= 16

    z, x, c = lax.axis_index("vocab"), lax.axis_index("rows"), lax.axis_index("teach")
    me = (z * nx + x) * nc + c

    def place(index):
        return {
            "vocab": lax.div(index, nx * nc),
            "rows": lax.rem(lax.div(index, nc), nx),
            "teach": lax.rem(index, nc),
        }

    def others(step):
        def run(offset, carry):
            step(lax.rem(me + offset, n))
            return carry

        lax.fori_loop(1, n, run, 0, unroll=unroll)

    w_copy = pltpu.make_async_copy(w_hbm, w, w_sem)
    w_copy.start()

    barrier = pltpu.get_barrier_semaphore()
    others(
        lambda d: pl.semaphore_signal(
            barrier, inc=1, device_id=place(d), device_id_type=pl.DeviceIdType.MESH
        )
    )

    hidden = hid[...].astype(jnp.float32)
    packed = jnp.concatenate([hidden[:, k * span:(k + 1) * span] for k in range(fold)], axis=0).astype(jnp.bfloat16)
    hsend[...] = packed
    hrecv[z] = packed
    low = mentor[:, :vocab]
    high = mentor[:, vocab:2 * vocab]
    first = c == 0
    mine = jnp.where(first, low, high)
    tsend[:, :vocab] = jnp.where(first, high, low)
    part[...] = jnp.zeros_like(part)

    pl.semaphore_wait(barrier, n - 1)

    def hidden_copy(zz):
        return pltpu.make_async_remote_copy(
            src_ref=hsend, dst_ref=hrecv.at[z], send_sem=hs_sem, recv_sem=hr_sem,
            device_id={"vocab": zz}, device_id_type=pl.DeviceIdType.MESH,
        )

    def send_hidden(offset, carry):
        hidden_copy(lax.rem(z + offset, nz)).start()
        return carry

    lax.fori_loop(1, nz, send_hidden, 0, unroll=nz <= 4)
    teacher_copy = pltpu.make_async_remote_copy(
        src_ref=tsend, dst_ref=trecv, send_sem=ts_sem, recv_sem=tr_sem,
        device_id={"teach": 1 - c}, device_id_type=pl.DeviceIdType.MESH,
    )
    teacher_copy.start()

    teacher_copy.wait_recv()
    theirs = trecv[:, :vocab]
    scaled = jnp.concatenate(
        [jnp.where(first, mine, theirs), jnp.where(first, theirs, mine)], axis=0
    ) * (1.0 / smoothing_divisor)
    max_t = jnp.max(scaled, axis=1, keepdims=True)
    weight_t = jnp.exp(scaled - max_t)
    sum_t = jnp.sum(weight_t, axis=1, keepdims=True)

    w_copy.wait()
    pltpu.make_async_copy(hrecv.at[pl.ds(0, nz - 1)], hrecv.at[pl.ds(0, nz - 1)], hr_sem).wait()
    arrived = [hrecv[k].astype(jnp.float32) for k in range(nz)]
    for k in range(fold):
        h[:, k * span:(k + 1) * span] = jnp.concatenate(
            [a[k * own:(k + 1) * own] for a in arrived], axis=0
        ).astype(jnp.bfloat16)

    student = dot(h[...], w[...], (1, 1)) * (1.0 / smoothing_divisor)
    max_s = jnp.max(student, axis=1, keepdims=True)
    sum_s = jnp.sum(jnp.exp(student - max_s), axis=1, keepdims=True)
    cross = jnp.sum(weight_t * (scaled - student), axis=1, keepdims=True)

    width = ssend.shape[1]
    line = column_to_row([max_s, max_t, sum_s, sum_t, cross], width)
    ssend[...] = line
    srecv[me] = line

    def stat_copy(d):
        return pltpu.make_async_remote_copy(
            src_ref=ssend, dst_ref=srecv.at[me], send_sem=ss_sem, recv_sem=sr_sem,
            device_id=place(d), device_id_type=pl.DeviceIdType.MESH,
        )

    others(lambda d: stat_copy(d).start())
    pltpu.make_async_copy(srecv.at[pl.ds(0, n - 1)], srecv.at[pl.ds(0, n - 1)], sr_sem).wait()
    stats = srecv[:, 0, :]
    top = jnp.max(stats, axis=0, keepdims=True)
    scale = jnp.exp(stats - top)
    lane = lax.broadcasted_iota(jnp.int32, stats.shape, 1)
    scale = jnp.where(lane < 4 * rows, pltpu.roll(scale, 2 * rows, 1), pltpu.roll(scale, 3 * rows, 1))
    sums = jnp.sum(stats * scale, axis=0, keepdims=True)
    all_max_s, all_max_t = row_to_column(top, 0, rows), row_to_column(top, 1, rows)
    all_sum_s, all_sum_t, all_cross = (row_to_column(sums, k, rows) for k in (2, 3, 4))
    lse_s = all_max_s + jnp.log(all_sum_s)
    lse_t = all_max_t + jnp.log(all_sum_t)
    keep = row_to_column(mask[...].astype(jnp.float32), 0, rows)
    div[...] = column_to_row([keep * (all_cross / all_sum_t - lse_t + lse_s)], rows)

    grad = (
        keep * (objective_scale * smoothing_divisor) * (jnp.exp(student - lse_s) - jnp.exp(scaled - lse_t))
    ).astype(jnp.bfloat16)

    for k in range(chunks):
        term = dot(grad, w[:, k * CHUNK:(k + 1) * CHUNK], (1, 0))
        for q in range(0, CHUNK, LANES):
            part[q // LANES, pl.ds(k, rows, stride=PACK), :] = term[:, q:q + LANES]
    for q in range(0, CHUNK, LANES):
        gsend[:, :, q:q + LANES] = part[q // LANES].reshape(rows, PACK, LANES).astype(jnp.bfloat16)
    grecv[me] = gsend[me]

    def grad_copy(d):
        return pltpu.make_async_remote_copy(
            src_ref=gsend.at[d], dst_ref=grecv.at[me], send_sem=gs_sem, recv_sem=gr_sem,
            device_id=place(d), device_id_type=pl.DeviceIdType.MESH,
        )

    others(lambda d: grad_copy(d).start())

    for k in range(0, depth, 2 * CHUNK):
        wg[:, k:k + 2 * CHUNK] = dot(grad, h[:, k:k + 2 * CHUNK], (0, 0)).astype(jnp.bfloat16)

    pltpu.make_async_copy(grecv.at[pl.ds(0, n - 1)], grecv.at[pl.ds(0, n - 1)], gr_sem).wait()
    total = jnp.sum(grecv[...].astype(jnp.float32), axis=0)
    for k in range(chunks):
        hg[:, k * CHUNK:(k + 1) * CHUNK] = total[k:k + 1].astype(jnp.bfloat16)

    pltpu.make_async_copy(hrecv.at[pl.ds(0, nz - 1)], hrecv.at[pl.ds(0, nz - 1)], hs_sem).wait()
    teacher_copy.wait_send()
    pltpu.make_async_copy(srecv.at[pl.ds(0, n - 1)], srecv.at[pl.ds(0, n - 1)], ss_sem).wait()
    pltpu.make_async_copy(grecv.at[pl.ds(0, n - 1)], grecv.at[pl.ds(0, n - 1)], gs_sem).wait()


def body(sizes, hidden_rows, mentor_unnormalized, head_weight, row_mask):
    nz, nx, nc = sizes
    n = nz * nx * nc
    own, depth = hidden_rows.shape
    vocab = head_weight.shape[0]
    rows = own * nz
    half = mentor_unnormalized.shape[0]
    assert rows == n and nc == 2 and PACK % own == 0 and depth % (2 * CHUNK) == 0 and depth // CHUNK <= PACK
    fold = PACK // own
    wide = -(-vocab // LANES) * LANES
    width = -(-5 * rows // LANES) * LANES
    vmem = pl.BlockSpec(memory_space=pltpu.VMEM)
    dma = pltpu.SemaphoreType.DMA
    wg, hg, div = pl.pallas_call(
        functools.partial(main_kernel, sizes),
        out_shape=(
            jax.ShapeDtypeStruct((vocab, depth), jnp.bfloat16),
            jax.ShapeDtypeStruct((1, depth), jnp.bfloat16),
            jax.ShapeDtypeStruct((1, rows), jnp.float32),
        ),
        in_specs=[vmem, vmem, pl.BlockSpec(memory_space=pl.ANY), vmem],
        out_specs=(vmem, vmem, vmem),
        scratch_shapes=[
            pltpu.VMEM((vocab, depth), jnp.bfloat16),
            pltpu.VMEM((PACK, depth // fold), jnp.bfloat16),
            pltpu.VMEM((nz, PACK, depth // fold), jnp.bfloat16),
            pltpu.VMEM((rows, depth), jnp.bfloat16),
            pltpu.VMEM((half, wide), jnp.float32),
            pltpu.VMEM((half, wide), jnp.float32),
            pltpu.VMEM((1, width), jnp.float32),
            pltpu.VMEM((n, 1, width), jnp.float32),
            pltpu.VMEM((CHUNK // LANES, rows * PACK, LANES), jnp.float32),
            pltpu.VMEM((rows, PACK, CHUNK), jnp.bfloat16),
            pltpu.VMEM((n, PACK, CHUNK), jnp.bfloat16),
        ] + [dma] * 9,
        compiler_params=pltpu.CompilerParams(
            collective_id=0, has_side_effects=True, vmem_limit_bytes=44 * 2**20
        ),
    )(hidden_rows, mentor_unnormalized, head_weight, row_mask.reshape(1, rows))
    return div.reshape(rows), hg, wg


def solution(mesh):
    sizes = (mesh.shape["vocab"], mesh.shape["rows"], mesh.shape["teach"])
    return jax.shard_map(
        functools.partial(body, sizes),
        mesh=mesh,
        in_specs=(
            P(("groups", "vocab"), None),
            P(("groups", "teach"), ("vocab", "rows")),
            P(("vocab", "rows", "teach"), None),
            P("groups"),
        ),
        out_specs=(
            P("groups"),
            P(("groups", "vocab", "rows", "teach"), None),
            P(("groups", "vocab", "rows", "teach"), None),
        ),
        check_vma=False,
    )
```

time: 149 us -> 27.5 us (0.18)
  blocking collectives: 135 us -> 0 us
  Pallas kernels: 0 us -> 20.2 us
  matrix products: 3.34 us -> 0 us
  starting transfers between devices: 3.25 us -> 0 us
  local copies, waits for them, and re-layouts: 3.85 us -> 6.19 us
  other arithmetic: 1.73 us -> 0 us
    psum x2 -> x0, blocking collectives: 89.4 us -> none  [body(): lax.psum((jnp.sum(jnp.exp(learner_unnormalized - max_student[:, None]), a...]
    pmax x1 -> x0, blocking collectives: 30.6 us -> none  [body(): lax.pmax((jnp.max(learner_unnormalized, axis=1), jnp.max(divided_learner_...]
    pallas_call x0 -> x1, Pallas kernels: none -> 20.2 us  [body(): pl.pallas_call(functools.partial(main_kernel, sizes), out_shape=(jax.Shap...]
    all_gather x1 -> x0, blocking collectives: 15.3 us -> none  [body(): gathered = lax.all_gather(hidden_rows, 'vocab', axis=0, tiled=True)]
    unnamed x8 -> x11, local copies, waits for them, and re-layouts: 0.72 us -> 6.19 us
    dot_general x3 -> x0, matrix products: 3.34 us -> none  [the longest x1 2.11 us: body(): lax.dot_general(raw_score_derivative, gathered, (((0,), (0,)), ((), ())),...]
    all_to_all x1 -> x0, starting transfers between devices: 3.25 us -> none  [body(): lax.all_to_all(mentor_unnormalized, 'teach', split_axis=1, concat_axis=0,...]
    all_to_all x2 -> x0, local copies, waits for them, and re-layouts: 1.57 us -> none  [body(): lax.all_to_all(mentor_unnormalized, 'teach', split_axis=1, concat_axis=0,...]
  transfers between devices with their start and end apart: 1 -> 0, of which waited for: 1 -> 0; matrix products, arithmetic and copies ran while one was open for 0% -> 0% of each run, Pallas kernels for 0% -> 0%
where the time goes in v1:
time: 27.5 us; the launch traced here: 27.1 us
  Pallas kernels  20.2 us (73%)
  local copies, waits for them, and re-layouts  6.19 us (23%)
  between operations  0.65 us (2%)
    pallas_call x1, Pallas kernels, body(): pl.pallas_call(functools.partial(main_kernel, sizes), out_shape=(jax.Shap...  20.2 us
    unnamed x11, local copies, waits for them, and re-layouts  6.19 us

profile of v1, /device:TPU:0, one launch (start us, length us, event | category | flops | bytes accessed | tf_op | source)
XLA Modules:
  0.0 27.1 jit_solution(4950549745030711097)
XLA Ops:
  0.6 0.0 copy-start
  0.6 1.6 %copy-done = bf16[304,3584]{1,0:T(8,128)(2,1)S(1)} copy-done((bf16[304,3584]{1,0:T(8,128)(2,1)S(1)}, bf16[304,3584]{1,0:T(8,128)(2,1)}, u32[]{:S(2)}) %copy-start) | copy-done | bytes 2179096
  2.2 0.0 copy-start.1
  2.2 0.7 %copy-done.1 = bf16[4,3584]{1,0:T(4,128)(2,1)S(1)} copy-done((bf16[4,3584]{1,0:T(4,128)(2,1)S(1)}, bf16[4,3584]{1,0:T(4,128)(2,1)}, u32[]{:S(2)}) %copy-start.1) | copy-done | bytes 28696
  3.0 0.0 copy-start.2
  3.0 0.7 %copy-done.2 = f32[8,608]{1,0:T(8,128)S(1)} copy-done((f32[8,608]{1,0:T(8,128)S(1)}, f32[8,608]{1,0:T(8,128)}, u32[]{:S(2)}) %copy-start.2) | copy-done | bytes 19480
  3.7 0.0 copy-start.3
  3.7 0.7 %copy-done.3 = s32[16]{0:T(128)S(1)} copy-done((s32[16]{0:T(128)S(1)}, s32[16]{0:T(128)}, u32[]{:S(2)}) %copy-start.3) | copy-done | bytes 88
  4.4 20.2 %shard_map.67 = (bf16[304,3584]{1,0:T(8,128)(2,1)S(1)}, bf16[1,3584]{1,0:T(2,128)(2,1)S(1)}, f32[1,16]{1,0:T(1,128)S(1)}) custom-call(bf16[4,3584]{1,0:T(4,128)(2,1)S(1)} %copy-done.1, f32[8,608]{1,0:T(8,128)S(1)} %copy-done.2, bf16[304,3584]{1,0:T(8,128)(2,1)S(1)} %copy-done, s32[1,16]{1,0:T(1,128)S(1)} %bitcast.2), custom_call_target="tpu_custom_call" | custom-call | tf_op jit(solution)/shard_map/pallas_call | solution.py:209
  24.6 0.5 %copy.10 = f32[16]{0:T(128)} copy(f32[16]{0:T(128)S(1)} %bitcast.3) | data formatting | bytes 128
  25.1 0.6 %copy.11 = bf16[1,3584]{1,0:T(2,128)(2,1)} copy(bf16[1,3584]{1,0:T(2,128)(2,1)S(1)} %get-tuple-element.13) | data formatting | bytes 14336
  25.7 1.3 %copy.12 = bf16[304,3584]{1,0:T(8,128)(2,1)} copy(bf16[304,3584]{1,0:T(8,128)(2,1)S(1)} %get-tuple-element.14) | data formatting | bytes 4358144
Async XLA Ops:
  0.6 1.6 %copy-start = (bf16[304,3584]{1,0:T(8,128)(2,1)S(1)}, bf16[304,3584]{1,0:T(8,128)(2,1)}, u32[]{:S(2)}) copy-start(bf16[304,3584]{1,0:T(8,128)(2,1)} %w_hbm.1) | copy-start | bytes 6537220
  2.2 0.7 %copy-start.1 = (bf16[4,3584]{1,0:T(4,128)(2,1)S(1)}, bf16[4,3584]{1,0:T(4,128)(2,1)}, u32[]{:S(2)}) copy-start(bf16[4,3584]{1,0:T(4,128)(2,1)} %hid.1) | copy-start | bytes 86020
  3.0 0.7 %copy-start.2 = (f32[8,608]{1,0:T(8,128)S(1)}, f32[8,608]{1,0:T(8,128)}, u32[]{:S(2)}) copy-start(f32[8,608]{1,0:T(8,128)} %mentor.1) | copy-start | bytes 58372
  3.7 0.7 %copy-start.3 = (s32[16]{0:T(128)S(1)}, s32[16]{0:T(128)}, u32[]{:S(2)}) copy-start(s32[16]{0:T(128)} %param.7) | copy-start | bytes 196

commit v2 on v1

v2 whole, which is shorter than its diff:
```python
import functools

import jax
import jax.numpy as jnp
from jax import lax
from jax.experimental import pallas as pl
from jax.experimental.pallas import tpu as pltpu
from jax.sharding import PartitionSpec as P

smoothing_divisor = 2.0
objective_scale = 256.0

LANES = 128
PACK = 16


def dot(a, b, contract):
    return lax.dot_general(a, b, ((contract[:1], contract[1:]), ((), ())), preferred_element_type=jnp.float32)


def column_to_row(columns, width):
    rows = columns[0].shape[0]
    lane = lax.broadcasted_iota(jnp.int32, (rows, width), 1)
    row = lax.broadcasted_iota(jnp.int32, (rows, width), 0)
    total = jnp.zeros((rows, width), jnp.float32)
    for place, column in enumerate(columns):
        total = jnp.where(lane == row + place * rows, column, total)
    return jnp.sum(total, axis=0, keepdims=True)


def row_to_column(line, place, rows):
    width = line.shape[1]
    lane = lax.broadcasted_iota(jnp.int32, (rows, width), 1)
    row = lax.broadcasted_iota(jnp.int32, (rows, width), 0)
    return jnp.sum(jnp.where(lane == row + place * rows, line, 0.0), axis=1, keepdims=True)


def main_kernel(
    sizes,
    hid_hbm, mentor_hbm, w_hbm, mask_hbm,
    wg, hg, div,
    hid, mentor, mask, w, hsend, hrecv, h, tsend, trecv, ssend, srecv, part, gsend, grecv,
    hid_sem, mentor_sem, mask_sem, w_sem,
    hs_sem, hr_sem, ts_sem, tr_sem, ss_sem, sr_sem, gs_sem, gr_sem,
):
    nz, nx, nc = sizes
    n = nz * nx * nc
    own, depth = hid.shape
    rows = own * nz
    vocab = w.shape[0]
    fold = PACK // own
    span = depth // fold
    halves = part.shape[0]
    reach = depth // halves
    unrolled = n <= 16

    z, x, c = lax.axis_index("vocab"), lax.axis_index("rows"), lax.axis_index("teach")
    me = (z * nx + x) * nc + c

    inputs = [
        pltpu.make_async_copy(hid_hbm, hid, hid_sem),
        pltpu.make_async_copy(mentor_hbm, mentor, mentor_sem),
        pltpu.make_async_copy(mask_hbm, mask, mask_sem),
        pltpu.make_async_copy(w_hbm, w, w_sem),
    ]
    for copy in inputs:
        copy.start()

    def others(step):
        if unrolled:
            zs = [z] + [lax.rem(z + k, nz) for k in range(1, nz)]
            xs = [x] + [lax.rem(x + k, nx) for k in range(1, nx)]
            cs = [c] + [lax.rem(c + k, nc) for k in range(1, nc)]
            for i in reversed(range(1, n)):
                zz, xx, cc = zs[i // (nx * nc)], xs[i // nc % nx], cs[i % nc]
                step((zz * nx + xx) * nc + cc, {"vocab": zz, "rows": xx, "teach": cc})
            return

        def run(offset, carry):
            d = lax.rem(me + offset, n)
            step(d, {
                "vocab": lax.div(d, nx * nc), "rows": lax.rem(lax.div(d, nc), nx), "teach": lax.rem(d, nc),
            })
            return carry

        lax.fori_loop(1, n, run, 0)

    barrier = pltpu.get_barrier_semaphore()
    others(
        lambda d, at: pl.semaphore_signal(
            barrier, inc=1, device_id=at, device_id_type=pl.DeviceIdType.MESH
        )
    )

    inputs[0].wait()
    hidden = hid[...].astype(jnp.float32)
    packed = jnp.concatenate([hidden[:, k * span:(k + 1) * span] for k in range(fold)], axis=0).astype(jnp.bfloat16)
    hsend[...] = packed
    hrecv[z] = packed
    inputs[1].wait()
    low = mentor[:, :vocab]
    high = mentor[:, vocab:2 * vocab]
    first = c == 0
    mine = jnp.where(first, low, high)
    tsend[:, :vocab] = jnp.where(first, high, low)
    part[...] = jnp.zeros_like(part)
    inputs[2].wait()
    keep = row_to_column(mask[...].astype(jnp.float32), 0, rows)

    pl.semaphore_wait(barrier, n - 1)

    def send_hidden(offset, carry):
        pltpu.make_async_remote_copy(
            src_ref=hsend, dst_ref=hrecv.at[z], send_sem=hs_sem, recv_sem=hr_sem,
            device_id={"vocab": lax.rem(z + offset, nz)}, device_id_type=pl.DeviceIdType.MESH,
        ).start()
        return carry

    teacher_copy = pltpu.make_async_remote_copy(
        src_ref=tsend, dst_ref=trecv, send_sem=ts_sem, recv_sem=tr_sem,
        device_id={"teach": 1 - c}, device_id_type=pl.DeviceIdType.MESH,
    )
    teacher_copy.start()
    lax.fori_loop(1, nz, send_hidden, 0, unroll=nz <= 4)

    teacher_copy.wait_recv()
    theirs = trecv[:, :vocab]
    scaled = jnp.concatenate(
        [jnp.where(first, mine, theirs), jnp.where(first, theirs, mine)], axis=0
    ) * (1.0 / smoothing_divisor)
    max_t = jnp.max(scaled, axis=1, keepdims=True)
    weight_t = jnp.exp(scaled - max_t)
    sum_t = jnp.sum(weight_t, axis=1, keepdims=True)

    inputs[3].wait()
    pltpu.make_async_copy(hrecv.at[pl.ds(0, nz - 1)], hrecv.at[pl.ds(0, nz - 1)], hr_sem).wait()
    arrived = [hrecv[k].astype(jnp.float32) for k in range(nz)]
    for k in range(fold):
        h[:, k * span:(k + 1) * span] = jnp.concatenate(
            [a[k * own:(k + 1) * own] for a in arrived], axis=0
        ).astype(jnp.bfloat16)

    student = dot(h[...], w[...], (1, 1)) * (1.0 / smoothing_divisor)
    max_s = jnp.max(student, axis=1, keepdims=True)
    sum_s = jnp.sum(jnp.exp(student - max_s), axis=1, keepdims=True)
    cross = jnp.sum(weight_t * (scaled - student), axis=1, keepdims=True)

    width = ssend.shape[1]
    line = column_to_row([max_s, max_t, sum_s, sum_t, cross], width)
    ssend[...] = line
    srecv[me] = line
    others(
        lambda d, at: pltpu.make_async_remote_copy(
            src_ref=ssend, dst_ref=srecv.at[me], send_sem=ss_sem, recv_sem=sr_sem,
            device_id=at, device_id_type=pl.DeviceIdType.MESH,
        ).start()
    )
    pltpu.make_async_copy(srecv.at[pl.ds(0, n - 1)], srecv.at[pl.ds(0, n - 1)], sr_sem).wait()
    stats = srecv[:, 0, :]
    top = jnp.max(stats, axis=0, keepdims=True)
    scale = jnp.exp(stats - top)
    lane = lax.broadcasted_iota(jnp.int32, stats.shape, 1)
    scale = jnp.where(lane < 4 * rows, pltpu.roll(scale, 2 * rows, 1), pltpu.roll(scale, 3 * rows, 1))
    sums = jnp.sum(stats * scale, axis=0, keepdims=True)
    all_max_s, all_max_t = row_to_column(top, 0, rows), row_to_column(top, 1, rows)
    all_sum_s, all_sum_t, all_cross = (row_to_column(sums, k, rows) for k in (2, 3, 4))
    lse_s = all_max_s + jnp.log(all_sum_s)
    lse_t = all_max_t + jnp.log(all_sum_t)

    grad = (
        keep * (objective_scale * smoothing_divisor) * (jnp.exp(student - lse_s) - jnp.exp(scaled - lse_t))
    ).astype(jnp.bfloat16)

    for s in range(halves):
        term = dot(grad, w[:, s * reach:(s + 1) * reach], (1, 0))
        for k in range(reach // LANES):
            part[s, pl.ds(k, rows, stride=PACK), :] = term[:, k * LANES:(k + 1) * LANES]
        gsend[s] = part[s].reshape(rows, PACK, LANES).astype(jnp.bfloat16)
        others(
            lambda d, at: pltpu.make_async_remote_copy(
                src_ref=gsend.at[s, d], dst_ref=grecv.at[s, me], send_sem=gs_sem.at[s], recv_sem=gr_sem.at[s],
                device_id=at, device_id_type=pl.DeviceIdType.MESH,
            ).start()
        )
        grecv[s, me] = gsend[s, me]

    div[...] = column_to_row([keep * (all_cross / all_sum_t - lse_t + lse_s)], rows)
    step = depth // 7 if depth % (7 * LANES) == 0 else LANES
    for k in range(0, depth, step):
        wg[:, k:k + step] = dot(grad, h[:, k:k + step], (0, 0)).astype(jnp.bfloat16)

    for s in range(halves):
        rest = grecv.at[s, pl.ds(0, n - 1)]
        pltpu.make_async_copy(rest, rest, gr_sem.at[s]).wait()
        total = jnp.sum(grecv[s].astype(jnp.float32), axis=0)
        for k in range(reach // LANES):
            at = s * reach + k * LANES
            hg[:, at:at + LANES] = total[k:k + 1].astype(jnp.bfloat16)

    pltpu.make_async_copy(hrecv.at[pl.ds(0, nz - 1)], hrecv.at[pl.ds(0, nz - 1)], hs_sem).wait()
    teacher_copy.wait_send()
    pltpu.make_async_copy(srecv.at[pl.ds(0, n - 1)], srecv.at[pl.ds(0, n - 1)], ss_sem).wait()
    for s in range(halves):
        rest = grecv.at[s, pl.ds(0, n - 1)]
        pltpu.make_async_copy(rest, rest, gs_sem.at[s]).wait()


def write_kernel(wg, hg, div, wg_out, hg_out, div_out, wg_sem, hg_sem, div_sem):
    copies = [
        pltpu.make_async_copy(wg, wg_out, wg_sem),
        pltpu.make_async_copy(hg, hg_out, hg_sem),
        pltpu.make_async_copy(div, div_out, div_sem),
    ]
    for copy in copies:
        copy.start()
    for copy in copies:
        copy.wait()


def body(sizes, hidden_rows, mentor_unnormalized, head_weight, row_mask):
    nz, nx, nc = sizes
    n = nz * nx * nc
    own, depth = hidden_rows.shape
    vocab = head_weight.shape[0]
    rows = own * nz
    half = mentor_unnormalized.shape[0]
    assert rows == n and nc == 2 and PACK % own == 0
    fold = PACK // own
    halves = 2
    assert depth % (halves * LANES) == 0 and depth // (halves * LANES) <= PACK
    wide = -(-vocab // LANES) * LANES
    width = -(-5 * rows // LANES) * LANES
    vmem = pl.BlockSpec(memory_space=pltpu.VMEM)
    hbm = pl.BlockSpec(memory_space=pltpu.HBM)
    dma = pltpu.SemaphoreType.DMA
    results = (
        jax.ShapeDtypeStruct((vocab, depth), jnp.bfloat16),
        jax.ShapeDtypeStruct((1, depth), jnp.bfloat16),
        jax.ShapeDtypeStruct((1, rows), jnp.float32),
    )
    made = pl.pallas_call(
        functools.partial(main_kernel, sizes),
        out_shape=results,
        in_specs=[hbm, hbm, hbm, hbm],
        out_specs=(vmem, vmem, vmem),
        scratch_shapes=[
            pltpu.VMEM((own, depth), jnp.bfloat16),
            pltpu.VMEM(mentor_unnormalized.shape, jnp.float32),
            pltpu.VMEM((1, rows), jnp.int32),
            pltpu.VMEM((vocab, depth), jnp.bfloat16),
            pltpu.VMEM((PACK, depth // fold), jnp.bfloat16),
            pltpu.VMEM((nz, PACK, depth // fold), jnp.bfloat16),
            pltpu.VMEM((rows, depth), jnp.bfloat16),
            pltpu.VMEM((half, wide), jnp.float32),
            pltpu.VMEM((half, wide), jnp.float32),
            pltpu.VMEM((1, width), jnp.float32),
            pltpu.VMEM((n, 1, width), jnp.float32),
            pltpu.VMEM((halves, rows * PACK, LANES), jnp.float32),
            pltpu.VMEM((halves, rows, PACK, LANES), jnp.bfloat16),
            pltpu.VMEM((halves, n, PACK, LANES), jnp.bfloat16),
        ] + [dma] * 10 + [dma((halves,))] * 2,
        compiler_params=pltpu.CompilerParams(
            collective_id=0, has_side_effects=True, vmem_limit_bytes=44 * 2**20
        ),
    )(*(
        pltpu.with_memory_space_constraint(a, pltpu.HBM)
        for a in (hidden_rows, mentor_unnormalized, head_weight, row_mask.reshape(1, rows))
    ))
    wg, hg, div = pl.pallas_call(
        write_kernel,
        out_shape=results,
        in_specs=[vmem, vmem, vmem],
        out_specs=(hbm, hbm, hbm),
        scratch_shapes=[dma] * 3,
    )(*made)
    return div.reshape(rows), hg, wg


def solution(mesh):
    sizes = (mesh.shape["vocab"], mesh.shape["rows"], mesh.shape["teach"])
    return jax.shard_map(
        functools.partial(body, sizes),
        mesh=mesh,
        in_specs=(
            P(("groups", "vocab"), None),
            P(("groups", "teach"), ("vocab", "rows")),
            P(("vocab", "rows", "teach"), None),
            P("groups"),
        ),
        out_specs=(
            P("groups"),
            P(("groups", "vocab", "rows", "teach"), None),
            P(("groups", "vocab", "rows", "teach"), None),
        ),
        check_vma=False,
    )
```

time: 27.5 us -> 27.4 us (level); the launches traced: 27.1 us -> 27.2 us
  Pallas kernels: 20.2 us -> 24.1 us
  local copies, waits for them, and re-layouts: 6.19 us -> 2.53 us
    pallas_call x1 -> x2, Pallas kernels: 20.2 us -> 24.1 us  [the longest x1 21.1 us: body(): pl.pallas_call(functools.partial(main_kernel, sizes), out_shape=results,...]
    unnamed x11 -> x6, local copies, waits for them, and re-layouts: 6.19 us -> 2.53 us
where the time goes in v2:
time: 27.4 us; the launch traced here: 27.2 us
  Pallas kernels  24.1 us (88%)
  local copies, waits for them, and re-layouts  2.53 us (9%)
  between operations  0.65 us (2%)
    pallas_call x1, Pallas kernels, body(): pl.pallas_call(functools.partial(main_kernel, sizes), out_shape=results,...  21.1 us
    pallas_call x1, Pallas kernels, body(): pl.pallas_call(write_kernel, out_shape=results, in_specs=[vmem, vmem, vme...  3.01 us
    unnamed x6, local copies, waits for them, and re-layouts  2.53 us

profile of v2, /device:TPU:0, one launch (start us, length us, event | category | flops | bytes accessed | tf_op | source)
XLA Modules:
  0.0 27.2 jit_solution(12678034909845323282)
XLA Ops:
  0.6 21.1 %shard_map.67 = (bf16[304,3584]{1,0:T(8,128)(2,1)S(1)}, bf16[1,3584]{1,0:T(2,128)(2,1)S(1)}, f32[1,16]{1,0:T(1,128)S(1)}) custom-call(bf16[4,3584]{1,0:T(4,128)(2,1)} %hid_hbm.1, f32[8,608]{1,0:T(8,128)} %mentor_hbm.1, bf16[304,3584]{1,0:T(8,128)(2,1)} %w_hbm.1, s32[1,16]{1,0:T(1,128)} %bitcast.2), custom_call_target="tpu_custom_call" | custom-call | tf_op jit(solution)/shard_map/pallas_call | solution.py:241
  21.7 0.0 copy-start
  21.7 1.4 %copy-done = bf16[304,3584]{1,0:T(8,128)(2,1)} copy-done((bf16[304,3584]{1,0:T(8,128)(2,1)}, bf16[304,3584]{1,0:T(8,128)(2,1)S(1)}, u32[]{:S(2)}) %copy-start) | copy-done | bytes 2179096
  23.1 0.0 copy-start.1
  23.1 0.6 %copy-done.1 = bf16[1,3584]{1,0:T(2,128)(2,1)} copy-done((bf16[1,3584]{1,0:T(2,128)(2,1)}, bf16[1,3584]{1,0:T(2,128)(2,1)S(1)}, u32[]{:S(2)}) %copy-start.1) | copy-done | bytes 7192
  23.7 0.0 copy-start.2
  23.7 0.6 %copy-done.2 = f32[1,16]{1,0:T(1,128)} copy-done((f32[1,16]{1,0:T(1,128)}, f32[1,16]{1,0:T(1,128)S(1)}, u32[]{:S(2)}) %copy-start.2) | copy-done | bytes 88
  24.2 3.0 %shard_map.68 = (bf16[304,3584]{1,0:T(8,128)(2,1)}, bf16[1,3584]{1,0:T(2,128)(2,1)}, f32[1,16]{1,0:T(1,128)}) custom-call(bf16[304,3584]{1,0:T(8,128)(2,1)} %copy-done, bf16[1,3584]{1,0:T(2,128)(2,1)} %copy-done.1, f32[1,16]{1,0:T(1,128)} %copy-done.2), custom_call_target="tpu_custom_call" | custom-call | tf_op jit(solution)/shard_map/pallas_call | solution.py:269
Async XLA Ops:
  21.7 1.4 %copy-start = (bf16[304,3584]{1,0:T(8,128)(2,1)}, bf16[304,3584]{1,0:T(8,128)(2,1)S(1)}, u32[]{:S(2)}) copy-start(bf16[304,3584]{1,0:T(8,128)(2,1)S(1)} %get-tuple-element.9.wg) | copy-start | bytes 6537220
  23.1 0.6 %copy-start.1 = (bf16[1,3584]{1,0:T(2,128)(2,1)}, bf16[1,3584]{1,0:T(2,128)(2,1)S(1)}, u32[]{:S(2)}) copy-start(bf16[1,3584]{1,0:T(2,128)(2,1)S(1)} %get-tuple-element.10.hg) | copy-start | bytes 21508
  23.7 0.6 %copy-start.2 = (f32[1,16]{1,0:T(1,128)}, f32[1,16]{1,0:T(1,128)S(1)}, u32[]{:S(2)}) copy-start(f32[1,16]{1,0:T(1,128)S(1)} %get-tuple-element.11.div) | copy-start | bytes 196

commit v3 on v2

--- a/solution.py
+++ b/solution.py
@@ -33,6 +33,19 @@
     lane = lax.broadcasted_iota(jnp.int32, (rows, width), 1)
     row = lax.broadcasted_iota(jnp.int32, (rows, width), 0)
     return jnp.sum(jnp.where(lane == row + place * rows, line, 0.0), axis=1, keepdims=True)
+
+
+def partners(index, size):
+    if size & (size - 1):
+        return [index] + [lax.rem(index + k, size) for k in range(1, size)]
+    result = []
+    for k in range(size):
+        value = index
+        for bit in range(size.bit_length() - 1):
+            if k >> bit & 1:
+                value = value + (1 - 2 * lax.rem(lax.div(index, 1 << bit), 2)) * (1 << bit)
+        result.append(value)
+    return result
 
 
 def main_kernel(
@@ -68,9 +81,7 @@
 
     def others(step):
         if unrolled:
-            zs = [z] + [lax.rem(z + k, nz) for k in range(1, nz)]
-            xs = [x] + [lax.rem(x + k, nx) for k in range(1, nx)]
-            cs = [c] + [lax.rem(c + k, nc) for k in range(1, nc)]
+            zs, xs, cs = partners(z, nz), partners(x, nx), partners(c, nc)
             for i in reversed(range(1, n)):
                 zz, xx, cc = zs[i // (nx * nc)], xs[i // nc % nx], cs[i % nc]
                 step((zz * nx + xx) * nc + cc, {"vocab": zz, "rows": xx, "teach": cc})
@@ -206,11 +217,12 @@
 
 
 def write_kernel(wg, hg, div, wg_out, hg_out, div_out, wg_sem, hg_sem, div_sem):
-    copies = [
-        pltpu.make_async_copy(wg, wg_out, wg_sem),
-        pltpu.make_async_copy(hg, hg_out, hg_sem),
-        pltpu.make_async_copy(div, div_out, div_sem),
-    ]
+    vocab = wg.shape[0]
+    slab = -(-vocab // (wg_sem.shape[0] * PACK)) * PACK
+    copies = [pltpu.make_async_copy(hg, hg_out, hg_sem), pltpu.make_async_copy(div, div_out, div_sem)]
+    for k, first in enumerate(range(0, vocab, slab)):
+        at = pl.ds(first, min(slab, vocab - first))
+        copies.append(pltpu.make_async_copy(wg.at[at], wg_out.at[at], wg_sem.at[k]))
     for copy in copies:
         copy.start()
     for copy in copies:
@@ -271,8 +283,9 @@
         out_shape=results,
         in_specs=[vmem, vmem, vmem],
         out_specs=(hbm, hbm, hbm),
-        scratch_shapes=[dma] * 3,
-    )(*made)
+        scratch_shapes=[dma((4,)), dma, dma],
+        compiler_params=pltpu.CompilerParams(vmem_limit_bytes=4 * 2**20),
+    )(*(pltpu.with_memory_space_constraint(a, pltpu.VMEM) for a in made))
     return div.reshape(rows), hg, wg
 
 

time: 27.4 us -> 23.2 us (0.85)
  local copies, waits for them, and re-layouts: 2.53 us -> 0 us
  Pallas kernels: 24.1 us -> 22.4 us
    unnamed x6 -> x0, local copies, waits for them, and re-layouts: 2.53 us -> none
    pallas_call x1, Pallas kernels: 3.01 us -> 1.4 us  [body(): pl.pallas_call(write_kernel, out_shape=results, in_specs=[vmem, vmem, vme...]
where the time goes in v3:
time: 23.2 us; the launch traced here: 23.1 us
  Pallas kernels  22.4 us (97%)
  between operations  0.64 us (3%)
    pallas_call x1, Pallas kernels, body(): pl.pallas_call(functools.partial(main_kernel, sizes), out_shape=results,...  21 us
    pallas_call x1, Pallas kernels, body(): pl.pallas_call(write_kernel, out_shape=results, in_specs=[vmem, vmem, vme...  1.4 us

profile of v3, /device:TPU:0, one launch (start us, length us, event | category | flops | bytes accessed | tf_op | source)
XLA Modules:
  0.0 23.1 jit_solution(15952598157326004544)
XLA Ops:
  0.6 21.0 %shard_map.67 = (bf16[304,3584]{1,0:T(8,128)(2,1)S(1)}, bf16[1,3584]{1,0:T(2,128)(2,1)S(1)}, f32[1,16]{1,0:T(1,128)S(1)}) custom-call(bf16[4,3584]{1,0:T(4,128)(2,1)} %hid_hbm.1, f32[8,608]{1,0:T(8,128)} %mentor_hbm.1, bf16[304,3584]{1,0:T(8,128)(2,1)} %w_hbm.1, s32[1,16]{1,0:T(1,128)} %bitcast.2), custom_call_target="tpu_custom_call" | custom-call | tf_op jit(solution)/shard_map/pallas_call | solution.py:253
  21.7 1.4 %shard_map.68 = (bf16[304,3584]{1,0:T(8,128)(2,1)}, bf16[1,3584]{1,0:T(2,128)(2,1)}, f32[1,16]{1,0:T(1,128)}) custom-call(bf16[304,3584]{1,0:T(8,128)(2,1)S(1)} %get-tuple-element.9.wg, bf16[1,3584]{1,0:T(2,128)(2,1)S(1)} %get-tuple-element.10.hg, f32[1,16]{1,0:T(1,128)S(1)} %get-tuple-element.11.div), custom_call_target="tpu_custom_call" | custom-call | tf_op jit(solution)/shard_map/pallas_call | solution.py:281

commit v4 on v3

--- a/solution.py
+++ b/solution.py
@@ -52,9 +52,9 @@
     sizes,
     hid_hbm, mentor_hbm, w_hbm, mask_hbm,
     wg, hg, div,
-    hid, mentor, mask, w, hsend, hrecv, h, tsend, trecv, ssend, srecv, part, gsend, grecv,
+    hid, mentor, mask, w, hsend, hrecv, h, tsend, trecv, ssend, srecv, part, theirs_part, gsend, grecv,
     hid_sem, mentor_sem, mask_sem, w_sem,
-    hs_sem, hr_sem, ts_sem, tr_sem, ss_sem, sr_sem, gs_sem, gr_sem,
+    hs_sem, hr_sem, ts_sem, tr_sem, ss_sem, sr_sem, ps_sem, pr_sem, gs_sem, gr_sem,
 ):
     nz, nx, nc = sizes
     n = nz * nx * nc
@@ -96,12 +96,33 @@
 
         lax.fori_loop(1, n, run, 0)
 
+    def same_core(step):
+        if unrolled:
+            zs, xs = partners(z, nz), partners(x, nx)
+            for i in reversed(range(1, nz * nx)):
+                zz, xx = zs[i // nx], xs[i % nx]
+                step(zz * nx + xx, {"vocab": zz, "rows": xx})
+            return
+
+        def run(offset, carry):
+            d = lax.rem(z * nx + x + offset, nz * nx)
+            step(d, {"vocab": lax.div(d, nx), "rows": lax.rem(d, nx)})
+            return carry
+
+        lax.fori_loop(1, nz * nx, run, 0)
+
     barrier = pltpu.get_barrier_semaphore()
-    others(
-        lambda d, at: pl.semaphore_signal(
-            barrier, inc=1, device_id=at, device_id_type=pl.DeviceIdType.MESH
-        )
-    )
+
+    def greet(at):
+        pl.semaphore_signal(barrier, inc=1, device_id=at, device_id_type=pl.DeviceIdType.MESH)
+
+    def greet_line(offset, carry):
+        greet({"vocab": lax.rem(z + offset, nz)})
+        return carry
+
+    lax.fori_loop(1, nz, greet_line, 0, unroll=nz <= 4)
+    for i in range(1, nx * nc):
+        greet({"rows": lax.rem(x + i // nc, nx), "teach": lax.rem(c + i % nc, nc)})
 
     inputs[0].wait()
     hidden = hid[...].astype(jnp.float32)
@@ -118,7 +139,7 @@
     inputs[2].wait()
     keep = row_to_column(mask[...].astype(jnp.float32), 0, rows)
 
-    pl.semaphore_wait(barrier, n - 1)
+    pl.semaphore_wait(barrier, nz - 1 + nx * nc - 1)
 
     def send_hidden(offset, carry):
         pltpu.make_async_remote_copy(
@@ -182,18 +203,32 @@
         keep * (objective_scale * smoothing_divisor) * (jnp.exp(student - lse_s) - jnp.exp(scaled - lse_t))
     ).astype(jnp.bfloat16)
 
+    chips = nz * nx
+    place = z * nx + x
+    swaps = []
     for s in range(halves):
         term = dot(grad, w[:, s * reach:(s + 1) * reach], (1, 0))
         for k in range(reach // LANES):
             part[s, pl.ds(k, rows, stride=PACK), :] = term[:, k * LANES:(k + 1) * LANES]
-        gsend[s] = part[s].reshape(rows, PACK, LANES).astype(jnp.bfloat16)
-        others(
+        swaps.append(pltpu.make_async_remote_copy(
+            src_ref=part.at[s].reshape(chips, nc, PACK, LANES).at[:, 1 - c], dst_ref=theirs_part.at[s],
+            send_sem=ps_sem.at[s], recv_sem=pr_sem.at[s],
+            device_id={"teach": 1 - c}, device_id_type=pl.DeviceIdType.MESH,
+        ))
+        swaps[-1].start()
+    for s in range(halves):
+        swaps[s].wait_recv()
+        both = part[s].reshape(chips, nc, PACK, LANES)
+        own_part = jnp.where(first, both[:, 0], both[:, 1])
+        gsend[s] = (own_part + theirs_part[s]).astype(jnp.bfloat16)
+        same_core(
             lambda d, at: pltpu.make_async_remote_copy(
-                src_ref=gsend.at[s, d], dst_ref=grecv.at[s, me], send_sem=gs_sem.at[s], recv_sem=gr_sem.at[s],
+                src_ref=gsend.at[s, d], dst_ref=grecv.at[s, place],
+                send_sem=gs_sem.at[s], recv_sem=gr_sem.at[s],
                 device_id=at, device_id_type=pl.DeviceIdType.MESH,
             ).start()
         )
-        grecv[s, me] = gsend[s, me]
+        grecv[s, place] = gsend[s, place]
 
     div[...] = column_to_row([keep * (all_cross / all_sum_t - lse_t + lse_s)], rows)
     step = depth // 7 if depth % (7 * LANES) == 0 else LANES
@@ -201,7 +236,7 @@
         wg[:, k:k + step] = dot(grad, h[:, k:k + step], (0, 0)).astype(jnp.bfloat16)
 
     for s in range(halves):
-        rest = grecv.at[s, pl.ds(0, n - 1)]
+        rest = grecv.at[s, pl.ds(0, chips - 1)]
         pltpu.make_async_copy(rest, rest, gr_sem.at[s]).wait()
         total = jnp.sum(grecv[s].astype(jnp.float32), axis=0)
         for k in range(reach // LANES):
@@ -210,9 +245,11 @@
 
     pltpu.make_async_copy(hrecv.at[pl.ds(0, nz - 1)], hrecv.at[pl.ds(0, nz - 1)], hs_sem).wait()
     teacher_copy.wait_send()
+    for swap in swaps:
+        swap.wait_send()
     pltpu.make_async_copy(srecv.at[pl.ds(0, n - 1)], srecv.at[pl.ds(0, n - 1)], ss_sem).wait()
     for s in range(halves):
-        rest = grecv.at[s, pl.ds(0, n - 1)]
+        rest = grecv.at[s, pl.ds(0, chips - 1)]
         pltpu.make_async_copy(rest, rest, gs_sem.at[s]).wait()
 
 
@@ -268,9 +305,10 @@
             pltpu.VMEM((1, width), jnp.float32),
             pltpu.VMEM((n, 1, width), jnp.float32),
             pltpu.VMEM((halves, rows * PACK, LANES), jnp.float32),
-            pltpu.VMEM((halves, rows, PACK, LANES), jnp.bfloat16),
-            pltpu.VMEM((halves, n, PACK, LANES), jnp.bfloat16),
-        ] + [dma] * 10 + [dma((halves,))] * 2,
+            pltpu.VMEM((halves, rows // nc, PACK, LANES), jnp.float32),
+            pltpu.VMEM((halves, rows // nc, PACK, LANES), jnp.bfloat16),
+            pltpu.VMEM((halves, rows // nc, PACK, LANES), jnp.bfloat16),
+        ] + [dma] * 10 + [dma((halves,))] * 4,
         compiler_params=pltpu.CompilerParams(
             collective_id=0, has_side_effects=True, vmem_limit_bytes=44 * 2**20
         ),

time: 23.2 us -> 22.2 us (0.957)
  Pallas kernels: 22.4 us -> 21.4 us
    pallas_call x1, Pallas kernels: 21 us -> 20 us  [body(): pl.pallas_call(functools.partial(main_kernel, sizes), out_shape=results,...]
where the time goes in v4:
time: 22.2 us; the launch traced here: 22 us
  Pallas kernels  21.4 us (96%)
  between operations  0.64 us (3%)
    pallas_call x1, Pallas kernels, body(): pl.pallas_call(functools.partial(main_kernel, sizes), out_shape=results,...  20 us
    pallas_call x1, Pallas kernels, body(): pl.pallas_call(write_kernel, out_shape=results, in_specs=[vmem, vmem, vme...  1.4 us

profile of v4, /device:TPU:0, one launch (start us, length us, event | category | flops | bytes accessed | tf_op | source)
XLA Modules:
  0.0 22.0 jit_solution(5989806838741329250)
XLA Ops:
  0.6 20.0 %shard_map.67 = (bf16[304,3584]{1,0:T(8,128)(2,1)S(1)}, bf16[1,3584]{1,0:T(2,128)(2,1)S(1)}, f32[1,16]{1,0:T(1,128)S(1)}) custom-call(bf16[4,3584]{1,0:T(4,128)(2,1)} %hid_hbm.1, f32[8,608]{1,0:T(8,128)} %mentor_hbm.1, bf16[304,3584]{1,0:T(8,128)(2,1)} %w_hbm.1, s32[1,16]{1,0:T(1,128)} %bitcast.2), custom_call_target="tpu_custom_call" | custom-call | tf_op jit(solution)/shard_map/pallas_call | solution.py:290
  20.6 1.4 %shard_map.68 = (bf16[304,3584]{1,0:T(8,128)(2,1)}, bf16[1,3584]{1,0:T(2,128)(2,1)}, f32[1,16]{1,0:T(1,128)}) custom-call(bf16[304,3584]{1,0:T(8,128)(2,1)S(1)} %get-tuple-element.9.wg, bf16[1,3584]{1,0:T(2,128)(2,1)S(1)} %get-tuple-element.10.hg, f32[1,16]{1,0:T(1,128)S(1)} %get-tuple-element.11.div), custom_call_target="tpu_custom_call" | custom-call | tf_op jit(solution)/shard_map/pallas_call | solution.py:319

commit v5 on v4

--- a/solution.py
+++ b/solution.py
@@ -52,9 +52,9 @@
     sizes,
     hid_hbm, mentor_hbm, w_hbm, mask_hbm,
     wg, hg, div,
-    hid, mentor, mask, w, hsend, hrecv, h, tsend, trecv, ssend, srecv, part, theirs_part, gsend, grecv,
+    hid, mentor, mask, w, hsend, direct, relayed, h, tsend, trecv, ssend, srecv, part, theirs_part, gsend, grecv,
     hid_sem, mentor_sem, mask_sem, w_sem,
-    hs_sem, hr_sem, ts_sem, tr_sem, ss_sem, sr_sem, ps_sem, pr_sem, gs_sem, gr_sem,
+    hs_sem, rs_sem, rr_sem, ts_sem, tr_sem, ss_sem, sr_sem, hr_sem, ps_sem, pr_sem, gs_sem, gr_sem,
 ):
     nz, nx, nc = sizes
     n = nz * nx * nc
@@ -124,36 +124,62 @@
     for i in range(1, nx * nc):
         greet({"rows": lax.rem(x + i // nc, nx), "teach": lax.rem(c + i % nc, nc)})
 
+    first = c == 0
+    piece = direct.shape[2]
+    rest_of = span - piece
     inputs[0].wait()
     hidden = hid[...].astype(jnp.float32)
     packed = jnp.concatenate([hidden[:, k * span:(k + 1) * span] for k in range(fold)], axis=0).astype(jnp.bfloat16)
-    hsend[...] = packed
-    hrecv[z] = packed
+    low, high = packed[:, :piece], packed[:, rest_of:]
+    hsend[...] = jnp.where(first, low, high)
+    direct[z] = jnp.where(first, low, high)
+    relayed[z] = jnp.where(first, high, low)
+
+    pl.semaphore_wait(barrier, nz - 1 + nx * nc - 1)
+
+    def send_hidden(to):
+        pltpu.make_async_remote_copy(
+            src_ref=hsend, dst_ref=direct.at[z], send_sem=hs_sem, recv_sem=hr_sem.at[z],
+            device_id={"vocab": to}, device_id_type=pl.DeviceIdType.MESH,
+        ).start()
+
+    def relay(source):
+        pltpu.make_async_copy(hsend, direct.at[source], hr_sem.at[source]).wait()
+        pltpu.make_async_remote_copy(
+            src_ref=direct.at[source], dst_ref=relayed.at[source], send_sem=rs_sem, recv_sem=rr_sem,
+            device_id={"teach": 1 - c}, device_id_type=pl.DeviceIdType.MESH,
+        ).start()
+
+    def line(step, far_first):
+        if unrolled:
+            peers = partners(z, nz)[1:]
+            for zz in reversed(peers) if far_first else peers:
+                step(zz)
+            return
+
+        def run(offset, carry):
+            step(lax.rem(z + offset, nz))
+            return carry
+
+        lax.fori_loop(1, nz, run, 0)
+
+    line(send_hidden, True)
+
     inputs[1].wait()
     low = mentor[:, :vocab]
     high = mentor[:, vocab:2 * vocab]
-    first = c == 0
     mine = jnp.where(first, low, high)
     tsend[:, :vocab] = jnp.where(first, high, low)
-    part[...] = jnp.zeros_like(part)
-    inputs[2].wait()
-    keep = row_to_column(mask[...].astype(jnp.float32), 0, rows)
-
-    pl.semaphore_wait(barrier, nz - 1 + nx * nc - 1)
-
-    def send_hidden(offset, carry):
-        pltpu.make_async_remote_copy(
-            src_ref=hsend, dst_ref=hrecv.at[z], send_sem=hs_sem, recv_sem=hr_sem,
-            device_id={"vocab": lax.rem(z + offset, nz)}, device_id_type=pl.DeviceIdType.MESH,
-        ).start()
-        return carry
-
     teacher_copy = pltpu.make_async_remote_copy(
         src_ref=tsend, dst_ref=trecv, send_sem=ts_sem, recv_sem=tr_sem,
         device_id={"teach": 1 - c}, device_id_type=pl.DeviceIdType.MESH,
     )
     teacher_copy.start()
-    lax.fori_loop(1, nz, send_hidden, 0, unroll=nz <= 4)
+    part[...] = jnp.zeros_like(part)
+    inputs[2].wait()
+    keep = row_to_column(mask[...].astype(jnp.float32), 0, rows)
+
+    line(relay, False)
 
     teacher_copy.wait_recv()
     theirs = trecv[:, :vocab]
@@ -165,8 +191,13 @@
     sum_t = jnp.sum(weight_t, axis=1, keepdims=True)
 
     inputs[3].wait()
-    pltpu.make_async_copy(hrecv.at[pl.ds(0, nz - 1)], hrecv.at[pl.ds(0, nz - 1)], hr_sem).wait()
-    arrived = [hrecv[k].astype(jnp.float32) for k in range(nz)]
+    peers = relayed.at[pl.ds(0, nz - 1)]
+    pltpu.make_async_copy(peers, peers, rr_sem).wait()
+    arrived = []
+    for k in range(nz):
+        low = jnp.where(first, direct[k], relayed[k])
+        high = jnp.where(first, relayed[k], direct[k])
+        arrived.append(jnp.concatenate([low, high[:, piece - rest_of:]], axis=1).astype(jnp.float32))
     for k in range(fold):
         h[:, k * span:(k + 1) * span] = jnp.concatenate(
             [a[k * own:(k + 1) * own] for a in arrived], axis=0
@@ -243,7 +274,8 @@
             at = s * reach + k * LANES
             hg[:, at:at + LANES] = total[k:k + 1].astype(jnp.bfloat16)
 
-    pltpu.make_async_copy(hrecv.at[pl.ds(0, nz - 1)], hrecv.at[pl.ds(0, nz - 1)], hs_sem).wait()
+    pltpu.make_async_copy(peers, peers, hs_sem).wait()
+    pltpu.make_async_copy(peers, peers, rs_sem).wait()
     teacher_copy.wait_send()
     for swap in swaps:
         swap.wait_send()
@@ -275,6 +307,8 @@
     half = mentor_unnormalized.shape[0]
     assert rows == n and nc == 2 and PACK % own == 0
     fold = PACK // own
+    assert depth % (fold * LANES) == 0
+    piece = -(-depth // (fold * nc * LANES)) * LANES
     halves = 2
     assert depth % (halves * LANES) == 0 and depth // (halves * LANES) <= PACK
     wide = -(-vocab // LANES) * LANES
@@ -297,8 +331,9 @@
             pltpu.VMEM(mentor_unnormalized.shape, jnp.float32),
             pltpu.VMEM((1, rows), jnp.int32),
             pltpu.VMEM((vocab, depth), jnp.bfloat16),
-            pltpu.VMEM((PACK, depth // fold), jnp.bfloat16),
-            pltpu.VMEM((nz, PACK, depth // fold), jnp.bfloat16),
+            pltpu.VMEM((PACK, piece), jnp.bfloat16),
+            pltpu.VMEM((nz, PACK, piece), jnp.bfloat16),
+            pltpu.VMEM((nz, PACK, piece), jnp.bfloat16),
             pltpu.VMEM((rows, depth), jnp.bfloat16),
             pltpu.VMEM((half, wide), jnp.float32),
             pltpu.VMEM((half, wide), jnp.float32),
@@ -308,7 +343,7 @@
             pltpu.VMEM((halves, rows // nc, PACK, LANES), jnp.float32),
             pltpu.VMEM((halves, rows // nc, PACK, LANES), jnp.bfloat16),
             pltpu.VMEM((halves, rows // nc, PACK, LANES), jnp.bfloat16),
-        ] + [dma] * 10 + [dma((halves,))] * 4,
+        ] + [dma] * 11 + [dma((nz,))] + [dma((halves,))] * 4,
         compiler_params=pltpu.CompilerParams(
             collective_id=0, has_side_effects=True, vmem_limit_bytes=44 * 2**20
         ),

time: 22.2 us -> 22 us (level)
  no operation moved by 1% of the time
where the time goes in v5:
time: 22 us; the launch traced here: 21.9 us
  Pallas kernels  21.2 us (96%)
  between operations  0.64 us (3%)
    pallas_call x1, Pallas kernels, body(): pl.pallas_call(functools.partial(main_kernel, sizes), out_shape=results,...  19.8 us
    pallas_call x1, Pallas kernels, body(): pl.pallas_call(write_kernel, out_shape=results, in_specs=[vmem, vmem, vme...  1.4 us

profile of v5, /device:TPU:0, one launch (start us, length us, event | category | flops | bytes accessed | tf_op | source)
XLA Modules:
  0.0 21.9 jit_solution(16435113111696465201)
XLA Ops:
  0.6 19.8 %shard_map.67 = (bf16[304,3584]{1,0:T(8,128)(2,1)S(1)}, bf16[1,3584]{1,0:T(2,128)(2,1)S(1)}, f32[1,16]{1,0:T(1,128)S(1)}) custom-call(bf16[4,3584]{1,0:T(4,128)(2,1)} %hid_hbm.1, f32[8,608]{1,0:T(8,128)} %mentor_hbm.1, bf16[304,3584]{1,0:T(8,128)(2,1)} %w_hbm.1, s32[1,16]{1,0:T(1,128)} %bitcast.2), custom_call_target="tpu_custom_call" | custom-call | tf_op jit(solution)/shard_map/pallas_call | solution.py:324
  20.5 1.4 %shard_map.68 = (bf16[304,3584]{1,0:T(8,128)(2,1)}, bf16[1,3584]{1,0:T(2,128)(2,1)}, f32[1,16]{1,0:T(1,128)}) custom-call(bf16[304,3584]{1,0:T(8,128)(2,1)S(1)} %get-tuple-element.9.wg, bf16[1,3584]{1,0:T(2,128)(2,1)S(1)} %get-tuple-element.10.hg, f32[1,16]{1,0:T(1,128)S(1)} %get-tuple-element.11.div), custom_call_target="tpu_custom_call" | custom-call | tf_op jit(solution)/shard_map/pallas_call | solution.py:354

commit v6 on v5

--- a/solution.py
+++ b/solution.py
@@ -191,21 +191,27 @@
     sum_t = jnp.sum(weight_t, axis=1, keepdims=True)
 
     inputs[3].wait()
+
+    def columns_of(held, k, start, width):
+        return jnp.concatenate(
+            [held[zz, :, pl.ds(start, width)][k * own:(k + 1) * own].astype(jnp.float32) for zz in range(nz)], axis=0
+        ).astype(jnp.bfloat16)
+
+    logits = jnp.zeros((rows, vocab), jnp.float32)
+    for k in range(fold):
+        at = pl.multiple_of(k * span + c * rest_of, LANES)
+        logits += dot(columns_of(direct, k, 0, piece), w[:, pl.ds(at, piece)], (1, 1))
     peers = relayed.at[pl.ds(0, nz - 1)]
     pltpu.make_async_copy(peers, peers, rr_sem).wait()
-    arrived = []
-    for k in range(nz):
-        low = jnp.where(first, direct[k], relayed[k])
-        high = jnp.where(first, relayed[k], direct[k])
-        arrived.append(jnp.concatenate([low, high[:, piece - rest_of:]], axis=1).astype(jnp.float32))
     for k in range(fold):
-        h[:, k * span:(k + 1) * span] = jnp.concatenate(
-            [a[k * own:(k + 1) * own] for a in arrived], axis=0
-        ).astype(jnp.bfloat16)
-
-    student = dot(h[...], w[...], (1, 1)) * (1.0 / smoothing_divisor)
+        start = pl.multiple_of((1 - c) * (piece - rest_of), LANES)
+        at = pl.multiple_of(k * span + (1 - c) * piece, LANES)
+        logits += dot(columns_of(relayed, k, start, rest_of), w[:, pl.ds(at, rest_of)], (1, 1))
+
+    student = logits * (1.0 / smoothing_divisor)
     max_s = jnp.max(student, axis=1, keepdims=True)
-    sum_s = jnp.sum(jnp.exp(student - max_s), axis=1, keepdims=True)
+    weight_s = jnp.exp(student - max_s)
+    sum_s = jnp.sum(weight_s, axis=1, keepdims=True)
     cross = jnp.sum(weight_t * (scaled - student), axis=1, keepdims=True)
 
     width = ssend.shape[1]
@@ -218,6 +224,15 @@
             device_id=at, device_id_type=pl.DeviceIdType.MESH,
         ).start()
     )
+    arrived = []
+    for k in range(nz):
+        low = jnp.where(first, direct[k], relayed[k])
+        high = jnp.where(first, relayed[k], direct[k])
+        arrived.append(jnp.concatenate([low, high[:, piece - rest_of:]], axis=1).astype(jnp.float32))
+    for k in range(fold):
+        h[:, k * span:(k + 1) * span] = jnp.concatenate(
+            [a[k * own:(k + 1) * own] for a in arrived], axis=0
+        ).astype(jnp.bfloat16)
     pltpu.make_async_copy(srecv.at[pl.ds(0, n - 1)], srecv.at[pl.ds(0, n - 1)], sr_sem).wait()
     stats = srecv[:, 0, :]
     top = jnp.max(stats, axis=0, keepdims=True)
@@ -230,8 +245,9 @@
     lse_s = all_max_s + jnp.log(all_sum_s)
     lse_t = all_max_t + jnp.log(all_sum_t)
 
+    factor = keep * (objective_scale * smoothing_divisor)
     grad = (
-        keep * (objective_scale * smoothing_divisor) * (jnp.exp(student - lse_s) - jnp.exp(scaled - lse_t))
+        weight_s * (factor * jnp.exp(max_s - lse_s)) - weight_t * (factor * jnp.exp(max_t - lse_t))
     ).astype(jnp.bfloat16)
 
     chips = nz * nx

time: 22 us -> 21.8 us (level)
    pallas_call x1, Pallas kernels: 19.8 us -> 19.6 us  [body(): pl.pallas_call(functools.partial(main_kernel, sizes), out_shape=results,...]
where the time goes in v6:
time: 21.8 us; the launch traced here: 21.6 us
  Pallas kernels  21 us (96%)
  between operations  0.64 us (3%)
    pallas_call x1, Pallas kernels, body(): pl.pallas_call(functools.partial(main_kernel, sizes), out_shape=results,...  19.6 us
    pallas_call x1, Pallas kernels, body(): pl.pallas_call(write_kernel, out_shape=results, in_specs=[vmem, vmem, vme...  1.4 us

profile of v6, /device:TPU:0, one launch (start us, length us, event | category | flops | bytes accessed | tf_op | source)
XLA Modules:
  0.0 21.6 jit_solution(13823453895141429914)
XLA Ops:
  0.6 19.6 %shard_map.67 = (bf16[304,3584]{1,0:T(8,128)(2,1)S(1)}, bf16[1,3584]{1,0:T(2,128)(2,1)S(1)}, f32[1,16]{1,0:T(1,128)S(1)}) custom-call(bf16[4,3584]{1,0:T(4,128)(2,1)} %hid_hbm.1, f32[8,608]{1,0:T(8,128)} %mentor_hbm.1, bf16[304,3584]{1,0:T(8,128)(2,1)} %w_hbm.1, s32[1,16]{1,0:T(1,128)} %bitcast.2), custom_call_target="tpu_custom_call" | custom-call | tf_op jit(solution)/shard_map/pallas_call | solution.py:340
  20.2 1.4 %shard_map.68 = (bf16[304,3584]{1,0:T(8,128)(2,1)}, bf16[1,3584]{1,0:T(2,128)(2,1)}, f32[1,16]{1,0:T(1,128)}) custom-call(bf16[304,3584]{1,0:T(8,128)(2,1)S(1)} %get-tuple-element.9.wg, bf16[1,3584]{1,0:T(2,128)(2,1)S(1)} %get-tuple-element.10.hg, f32[1,16]{1,0:T(1,128)S(1)} %get-tuple-element.11.div), custom_call_target="tpu_custom_call" | custom-call | tf_op jit(solution)/shard_map/pallas_call | solution.py:370

commit v7 on v3

v7 whole, which is shorter than its diff:
```python
import functools

import jax
import jax.numpy as jnp
from jax import lax
from jax.experimental import pallas as pl
from jax.experimental.pallas import tpu as pltpu
from jax.sharding import PartitionSpec as P

smoothing_divisor = 2.0
objective_scale = 256.0

LANES = 128
PACK = 16


def dot(a, b, contract):
    return lax.dot_general(a, b, ((contract[:1], contract[1:]), ((), ())), preferred_element_type=jnp.float32)


def column_to_row(columns, width):
    rows = columns[0].shape[0]
    lane = lax.broadcasted_iota(jnp.int32, (rows, width), 1)
    row = lax.broadcasted_iota(jnp.int32, (rows, width), 0)
    total = jnp.zeros((rows, width), jnp.float32)
    for place, column in enumerate(columns):
        total = jnp.where(lane == row + place * rows, column, total)
    return jnp.sum(total, axis=0, keepdims=True)


def row_to_column(line, place, rows):
    width = line.shape[1]
    lane = lax.broadcasted_iota(jnp.int32, (rows, width), 1)
    row = lax.broadcasted_iota(jnp.int32, (rows, width), 0)
    return jnp.sum(jnp.where(lane == row + place * rows, line, 0.0), axis=1, keepdims=True)


def partners(index, size):
    if size & (size - 1):
        return [index] + [lax.rem(index + k, size) for k in range(1, size)]
    result = []
    for k in range(size):
        value = index
        for bit in range(size.bit_length() - 1):
            if k >> bit & 1:
                value = value + (1 - 2 * lax.rem(lax.div(index, 1 << bit), 2)) * (1 << bit)
        result.append(value)
    return result


def main_kernel(
    sizes,
    hid_hbm, mentor_hbm, w_hbm, mask_hbm,
    wg, hg, div,
    hid, mentor, mask, w, w_other, hsend, held, held_other, h, gx, gx_other, ssend, srecv, part, gsend, grecv,
    hid_sem, mentor_sem, mask_sem, w_sem,
    ws_sem, wr_sem, xs_sem, xr_sem, ts_sem, tr_sem, ss_sem, sr_sem, hs_sem, hr_sem, gs_sem, gr_sem,
):
    nz, nx, nc = sizes
    chips = nz * nx
    sources = nz // nc
    own, depth = hid.shape
    half = own * sources
    rows = half * nc
    vocab = w.shape[0]
    fold = PACK // own
    span = depth // fold
    halves = part.shape[0]
    reach = depth // halves
    unrolled = chips <= 8

    z, x, c = lax.axis_index("vocab"), lax.axis_index("rows"), lax.axis_index("teach")
    place = z * nx + x
    me = place * nc + c
    first = c == 0
    mine_is_source = lax.div(z, sources) == c
    mine_is_owner = lax.div(me, half) == c

    def same_core(step):
        if unrolled:
            zs, xs = partners(z, nz), partners(x, nx)
            for i in reversed(range(1, chips)):
                zz, xx = zs[i // nx], xs[i % nx]
                step(zz * nx + xx, {"vocab": zz, "rows": xx})
            return

        def run(offset, carry):
            d = lax.rem(place + offset, chips)
            step(d, {"vocab": lax.div(d, nx), "rows": lax.rem(d, nx)})
            return carry

        lax.fori_loop(1, chips, run, 0)

    barrier = pltpu.get_barrier_semaphore()

    def greet(at):
        pl.semaphore_signal(barrier, inc=1, device_id=at, device_id_type=pl.DeviceIdType.MESH)

    same_core(lambda d, at: greet(at))
    greet({"teach": 1 - c})

    inputs = [
        pltpu.make_async_copy(hid_hbm, hid, hid_sem),
        pltpu.make_async_copy(mentor_hbm, mentor, mentor_sem),
        pltpu.make_async_copy(mask_hbm, mask, mask_sem),
        pltpu.make_async_copy(w_hbm, w, w_sem),
    ]
    for copy in inputs:
        copy.start()

    inputs[0].wait()
    hidden = hid[...].astype(jnp.float32)
    hsend[...] = jnp.concatenate(
        [hidden[:, k * span:(k + 1) * span] for k in range(fold)], axis=0
    ).astype(jnp.bfloat16)

    pl.semaphore_wait(barrier, chips)

    slot = lax.rem(z, sources)

    @pl.when(mine_is_source)
    def _():
        held[slot] = hsend[...]

        def send_hidden(offset, carry):
            pltpu.make_async_remote_copy(
                src_ref=hsend, dst_ref=held.at[slot], send_sem=hs_sem.at[offset], recv_sem=hr_sem.at[slot],
                device_id={"vocab": lax.rem(z + offset, nz)}, device_id_type=pl.DeviceIdType.MESH,
            ).start()
            return carry

        lax.fori_loop(1, nz, send_hidden, 0, unroll=nz <= 4)

    inputs[3].wait()
    sibling = {"teach": 1 - c}
    w_swap = pltpu.make_async_remote_copy(
        src_ref=w, dst_ref=w_other, send_sem=ws_sem, recv_sem=wr_sem,
        device_id=sibling, device_id_type=pl.DeviceIdType.MESH,
    )
    w_swap.start()

    inputs[1].wait()
    low = mentor[:, :vocab] * (1.0 / smoothing_divisor)
    high = mentor[:, vocab:2 * vocab] * (1.0 / smoothing_divisor)
    scaled = [jnp.where(first, low, high), jnp.where(first, high, low)]

    def largest(pair):
        return jnp.maximum(jnp.max(pair[0], axis=1, keepdims=True), jnp.max(pair[1], axis=1, keepdims=True))

    def added(pair):
        return jnp.sum(pair[0], axis=1, keepdims=True) + jnp.sum(pair[1], axis=1, keepdims=True)

    max_t = largest(scaled)
    weight_t = [jnp.exp(v - max_t) for v in scaled]
    sum_t = added(weight_t)
    part[...] = jnp.zeros_like(part)
    inputs[2].wait()
    keep = row_to_column(mask[...].astype(jnp.float32), c, half)

    for source in range(sources):
        @pl.when(jnp.logical_not(jnp.logical_and(mine_is_source, slot == source)))
        def _():
            pltpu.make_async_copy(hsend, held.at[source], hr_sem.at[source]).wait()

    h_swap = pltpu.make_async_remote_copy(
        src_ref=held, dst_ref=held_other, send_sem=xs_sem, recv_sem=xr_sem,
        device_id=sibling, device_id_type=pl.DeviceIdType.MESH,
    )
    h_swap.start()

    def whole(blocks):
        wide = [blocks[k].astype(jnp.float32) for k in range(sources)]
        return jnp.concatenate(
            [jnp.concatenate([a[k * own:(k + 1) * own] for a in wide], axis=0) for k in range(fold)], axis=1
        )

    mine_h = whole(held)
    mine_b = mine_h.astype(jnp.bfloat16)
    student_own = dot(mine_b, w[...], (1, 1)) * (1.0 / smoothing_divisor)
    w_swap.wait_recv()
    student = [student_own, dot(mine_b, w_other[...], (1, 1)) * (1.0 / smoothing_divisor)]
    max_s = largest(student)
    weight_s = [jnp.exp(v - max_s) for v in student]
    sum_s = added(weight_s)
    cross = added([p * (t - v) for p, t, v in zip(weight_t, scaled, student)])

    width = ssend.shape[1]
    line = column_to_row([max_s, max_t, sum_s, sum_t, cross], width)
    ssend[...] = line
    srecv[place] = line
    same_core(
        lambda d, at: pltpu.make_async_remote_copy(
            src_ref=ssend, dst_ref=srecv.at[place], send_sem=ss_sem, recv_sem=sr_sem,
            device_id=at, device_id_type=pl.DeviceIdType.MESH,
        ).start()
    )
    h_swap.wait_recv()
    theirs_h = whole(held_other)
    h[...] = jnp.concatenate(
        [jnp.where(first, mine_h, theirs_h), jnp.where(first, theirs_h, mine_h)], axis=0
    ).astype(jnp.bfloat16)
    rest = srecv.at[pl.ds(0, chips - 1)]
    pltpu.make_async_copy(rest, rest, sr_sem).wait()
    stats = srecv[:, 0, :]
    top = jnp.max(stats, axis=0, keepdims=True)
    scale = jnp.exp(stats - top)
    lane = lax.broadcasted_iota(jnp.int32, stats.shape, 1)
    scale = jnp.where(lane < 4 * half, pltpu.roll(scale, 2 * half, 1), pltpu.roll(scale, 3 * half, 1))
    sums = jnp.sum(stats * scale, axis=0, keepdims=True)
    all_max_s, all_max_t = row_to_column(top, 0, half), row_to_column(top, 1, half)
    all_sum_s, all_sum_t, all_cross = (row_to_column(sums, k, half) for k in (2, 3, 4))
    lse_s = all_max_s + jnp.log(all_sum_s)
    lse_t = all_max_t + jnp.log(all_sum_t)

    factor = keep * (objective_scale * smoothing_divisor)
    factor_s, factor_t = factor * jnp.exp(max_s - lse_s), factor * jnp.exp(max_t - lse_t)
    grad = [(s * factor_s - t * factor_t).astype(jnp.bfloat16) for s, t in zip(weight_s, weight_t)]

    mine_div = keep * (all_cross / all_sum_t - lse_t + lse_s)
    gx[:, :vocab] = grad[1].astype(jnp.float32)
    gx[:, vocab:vocab + 1] = mine_div
    g_swap = pltpu.make_async_remote_copy(
        src_ref=gx, dst_ref=gx_other, send_sem=ts_sem, recv_sem=tr_sem,
        device_id=sibling, device_id_type=pl.DeviceIdType.MESH,
    )
    g_swap.start()

    for s in range(halves):
        columns = slice(s * reach, (s + 1) * reach)
        term = dot(grad[0], w[:, columns], (1, 0)) + dot(grad[1], w_other[:, columns], (1, 0))
        for k in range(reach // LANES):
            part[s, pl.ds(k, half, stride=PACK), :] = term[:, k * LANES:(k + 1) * LANES]
        gsend[s] = part[s].reshape(half, PACK, LANES).astype(jnp.bfloat16)

        def send_row(r, carry):
            owner = c * half + r

            @pl.when(owner != me)
            def _():
                pltpu.make_async_remote_copy(
                    src_ref=gsend.at[s, r], dst_ref=grecv.at[s, place],
                    send_sem=gs_sem.at[s], recv_sem=gr_sem.at[s],
                    device_id={
                        "vocab": lax.div(owner, nx * nc), "rows": lax.rem(lax.div(owner, nc), nx),
                        "teach": lax.rem(owner, nc),
                    },
                    device_id_type=pl.DeviceIdType.MESH,
                ).start()

            return carry

        lax.fori_loop(0, half, send_row, 0, unroll=unrolled)

        @pl.when(mine_is_owner)
        def _():
            grecv[s, place] = gsend[s, lax.rem(me, half)]

    g_swap.wait_recv()
    theirs = gx_other[:, :vocab]
    own_grad = grad[0].astype(jnp.float32)
    both = jnp.concatenate(
        [jnp.where(first, own_grad, theirs), jnp.where(first, theirs, own_grad)], axis=0
    ).astype(jnp.bfloat16)
    theirs_div = gx_other[:, vocab:vocab + 1]
    div[...] = column_to_row(
        [jnp.where(first, mine_div, theirs_div), jnp.where(first, theirs_div, mine_div)], rows
    )
    step = depth // 7 if depth % (7 * LANES) == 0 else LANES
    for k in range(0, depth, step):
        wg[:, k:k + step] = dot(both, h[:, k:k + step], (0, 0)).astype(jnp.bfloat16)

    def settle(s, sem):
        @pl.when(mine_is_owner)
        def _():
            rest = grecv.at[s, pl.ds(0, chips - 1)]
            pltpu.make_async_copy(rest, rest, sem).wait()

        @pl.when(jnp.logical_not(mine_is_owner))
        def _():
            pltpu.make_async_copy(grecv.at[s], grecv.at[s], sem).wait()

    for s in range(halves):
        settle(s, gr_sem.at[s])
        total = jnp.sum(grecv[s].astype(jnp.float32), axis=0)
        for k in range(reach // LANES):
            at = s * reach + k * LANES
            hg[:, at:at + LANES] = total[k:k + 1].astype(jnp.bfloat16)

    @pl.when(mine_is_source)
    def _():
        def sent(offset, carry):
            pltpu.make_async_copy(hsend, hsend, hs_sem.at[offset]).wait()
            return carry

        lax.fori_loop(1, nz, sent, 0)

    for swap in (w_swap, h_swap, g_swap):
        swap.wait_send()
    rest = srecv.at[pl.ds(0, chips - 1)]
    pltpu.make_async_copy(rest, rest, ss_sem).wait()
    for s in range(halves):
        settle(s, gs_sem.at[s])


def write_kernel(wg, hg, div, wg_out, hg_out, div_out, wg_sem, hg_sem, div_sem):
    vocab = wg.shape[0]
    slab = -(-vocab // (wg_sem.shape[0] * PACK)) * PACK
    copies = [pltpu.make_async_copy(hg, hg_out, hg_sem), pltpu.make_async_copy(div, div_out, div_sem)]
    for k, first in enumerate(range(0, vocab, slab)):
        at = pl.ds(first, min(slab, vocab - first))
        copies.append(pltpu.make_async_copy(wg.at[at], wg_out.at[at], wg_sem.at[k]))
    for copy in copies:
        copy.start()
    for copy in copies:
        copy.wait()


def body(sizes, hidden_rows, mentor_unnormalized, head_weight, row_mask):
    nz, nx, nc = sizes
    n = nz * nx * nc
    own, depth = hidden_rows.shape
    vocab = head_weight.shape[0]
    rows = own * nz
    half = mentor_unnormalized.shape[0]
    assert rows == n and nc == 2 and nz % nc == 0 and half == rows // nc
    assert PACK % own == 0 and depth % (PACK // own * LANES) == 0
    fold = PACK // own
    chips = nz * nx
    sources = nz // nc
    span = depth // fold
    halves = 2
    assert depth % (halves * LANES) == 0 and depth // (halves * LANES) <= PACK
    wide = -(-(vocab + 1) // LANES) * LANES
    width = -(-5 * half // LANES) * LANES
    vmem = pl.BlockSpec(memory_space=pltpu.VMEM)
    hbm = pl.BlockSpec(memory_space=pltpu.HBM)
    dma = pltpu.SemaphoreType.DMA
    results = (
        jax.ShapeDtypeStruct((vocab, depth), jnp.bfloat16),
        jax.ShapeDtypeStruct((1, depth), jnp.bfloat16),
        jax.ShapeDtypeStruct((1, rows), jnp.float32),
    )
    made = pl.pallas_call(
        functools.partial(main_kernel, sizes),
        out_shape=results,
        in_specs=[hbm, hbm, hbm, hbm],
        out_specs=(vmem, vmem, vmem),
        scratch_shapes=[
            pltpu.VMEM((own, depth), jnp.bfloat16),
            pltpu.VMEM(mentor_unnormalized.shape, jnp.float32),
            pltpu.VMEM((1, rows), jnp.int32),
            pltpu.VMEM((vocab, depth), jnp.bfloat16),
            pltpu.VMEM((vocab, depth), jnp.bfloat16),
            pltpu.VMEM((PACK, span), jnp.bfloat16),
            pltpu.VMEM((sources, PACK, span), jnp.bfloat16),
            pltpu.VMEM((sources, PACK, span), jnp.bfloat16),
            pltpu.VMEM((rows, depth), jnp.bfloat16),
            pltpu.VMEM((half, wide), jnp.float32),
            pltpu.VMEM((half, wide), jnp.float32),
            pltpu.VMEM((1, width), jnp.float32),
            pltpu.VMEM((chips, 1, width), jnp.float32),
            pltpu.VMEM((halves, half * PACK, LANES), jnp.float32),
            pltpu.VMEM((halves, half, PACK, LANES), jnp.bfloat16),
            pltpu.VMEM((halves, chips, PACK, LANES), jnp.bfloat16),
        ] + [dma] * 12 + [dma((nz,)), dma((sources,))] + [dma((halves,))] * 2,
        compiler_params=pltpu.CompilerParams(
            collective_id=0, has_side_effects=True, vmem_limit_bytes=44 * 2**20
        ),
    )(*(
        pltpu.with_memory_space_constraint(a, pltpu.HBM)
        for a in (hidden_rows, mentor_unnormalized, head_weight, row_mask.reshape(1, rows))
    ))
    wg, hg, div = pl.pallas_call(
        write_kernel,
        out_shape=results,
        in_specs=[vmem, vmem, vmem],
        out_specs=(hbm, hbm, hbm),
        scratch_shapes=[dma((4,)), dma, dma],
        compiler_params=pltpu.CompilerParams(vmem_limit_bytes=4 * 2**20),
    )(*(pltpu.with_memory_space_constraint(a, pltpu.VMEM) for a in made))
    return div.reshape(rows), hg, wg


def solution(mesh):
    sizes = (mesh.shape["vocab"], mesh.shape["rows"], mesh.shape["teach"])
    return jax.shard_map(
        functools.partial(body, sizes),
        mesh=mesh,
        in_specs=(
            P(("groups", "vocab"), None),
            P(("groups", "teach"), ("vocab", "rows")),
            P(("vocab", "rows", "teach"), None),
            P("groups"),
        ),
        out_specs=(
            P("groups"),
            P(("groups", "vocab", "rows", "teach"), None),
            P(("groups", "vocab", "rows", "teach"), None),
        ),
        check_vma=False,
    )
```

time: 23.2 us -> 23.5 us (1.013)
  Pallas kernels: 22.4 us -> 22.7 us
where the time goes in v7:
time: 23.5 us; the launch traced here: 23.3 us
  Pallas kernels  22.7 us (97%)
  between operations  0.64 us (3%)
    pallas_call x1, Pallas kernels, body(): pl.pallas_call(functools.partial(main_kernel, sizes), out_shape=results,...  21.3 us
    pallas_call x1, Pallas kernels, body(): pl.pallas_call(write_kernel, out_shape=results, in_specs=[vmem, vmem, vme...  1.4 us

profile of v7, /device:TPU:0, one launch (start us, length us, event | category | flops | bytes accessed | tf_op | source)
XLA Modules:
  0.0 23.3 jit_solution(1276378942528278038)
XLA Ops:
  0.6 21.3 %shard_map.67 = (bf16[304,3584]{1,0:T(8,128)(2,1)S(1)}, bf16[1,3584]{1,0:T(2,128)(2,1)S(1)}, f32[1,16]{1,0:T(1,128)S(1)}) custom-call(bf16[4,3584]{1,0:T(4,128)(2,1)} %hid_hbm.1, f32[8,608]{1,0:T(8,128)} %mentor_hbm.1, bf16[304,3584]{1,0:T(8,128)(2,1)} %w_hbm.1, s32[1,16]{1,0:T(1,128)} %bitcast.2), custom_call_target="tpu_custom_call" | custom-call | tf_op jit(solution)/shard_map/pallas_call | solution.py:343
  21.9 1.4 %shard_map.68 = (bf16[304,3584]{1,0:T(8,128)(2,1)}, bf16[1,3584]{1,0:T(2,128)(2,1)}, f32[1,16]{1,0:T(1,128)}) custom-call(bf16[304,3584]{1,0:T(8,128)(2,1)S(1)} %get-tuple-element.9.wg, bf16[1,3584]{1,0:T(2,128)(2,1)S(1)} %get-tuple-element.10.hg, f32[1,16]{1,0:T(1,128)S(1)} %get-tuple-element.11.div), custom_call_target="tpu_custom_call" | custom-call | tf_op jit(solution)/shard_map/pallas_call | solution.py:373

commit v8 on v6

--- a/solution.py
+++ b/solution.py
@@ -70,6 +70,51 @@
     z, x, c = lax.axis_index("vocab"), lax.axis_index("rows"), lax.axis_index("teach")
     me = (z * nx + x) * nc + c
 
+    def others(step):
+        if unrolled:
+            zs, xs, cs = partners(z, nz), partners(x, nx), partners(c, nc)
+            for i in reversed(range(1, n)):
+                zz, xx, cc = zs[i // (nx * nc)], xs[i // nc % nx], cs[i % nc]
+                step((zz * nx + xx) * nc + cc, {"vocab": zz, "rows": xx, "teach": cc})
+            return
+
+        def run(offset, carry):
+            d = lax.rem(me + offset, n)
+            step(d, {
+                "vocab": lax.div(d, nx * nc), "rows": lax.rem(lax.div(d, nc), nx), "teach": lax.rem(d, nc),
+            })
+            return carry
+
+        lax.fori_loop(1, n, run, 0)
+
+    def same_core(step):
+        if unrolled:
+            zs, xs = partners(z, nz), partners(x, nx)
+            for i in reversed(range(1, nz * nx)):
+                zz, xx = zs[i // nx], xs[i % nx]
+                step(zz * nx + xx, {"vocab": zz, "rows": xx})
+            return
+
+        def run(offset, carry):
+            d = lax.rem(z * nx + x + offset, nz * nx)
+            step(d, {"vocab": lax.div(d, nx), "rows": lax.rem(d, nx)})
+            return carry
+
+        lax.fori_loop(1, nz * nx, run, 0)
+
+    barrier = pltpu.get_barrier_semaphore()
+
+    def greet(at):
+        pl.semaphore_signal(barrier, inc=1, device_id=at, device_id_type=pl.DeviceIdType.MESH)
+
+    def greet_line(offset, carry):
+        greet({"vocab": lax.rem(z + offset, nz)})
+        return carry
+
+    lax.fori_loop(1, nz, greet_line, 0, unroll=nz <= 4)
+    for i in range(1, nx * nc):
+        greet({"rows": lax.rem(x + i // nc, nx), "teach": lax.rem(c + i % nc, nc)})
+
     inputs = [
         pltpu.make_async_copy(hid_hbm, hid, hid_sem),
         pltpu.make_async_copy(mentor_hbm, mentor, mentor_sem),
@@ -78,51 +123,6 @@
     ]
     for copy in inputs:
         copy.start()
-
-    def others(step):
-        if unrolled:
-            zs, xs, cs = partners(z, nz), partners(x, nx), partners(c, nc)
-            for i in reversed(range(1, n)):
-                zz, xx, cc = zs[i // (nx * nc)], xs[i // nc % nx], cs[i % nc]
-                step((zz * nx + xx) * nc + cc, {"vocab": zz, "rows": xx, "teach": cc})
-            return
-
-        def run(offset, carry):
-            d = lax.rem(me + offset, n)
-            step(d, {
-                "vocab": lax.div(d, nx * nc), "rows": lax.rem(lax.div(d, nc), nx), "teach": lax.rem(d, nc),
-            })
-            return carry
-
-        lax.fori_loop(1, n, run, 0)
-
-    def same_core(step):
-        if unrolled:
-            zs, xs = partners(z, nz), partners(x, nx)
-            for i in reversed(range(1, nz * nx)):
-                zz, xx = zs[i // nx], xs[i % nx]
-                step(zz * nx + xx, {"vocab": zz, "rows": xx})
-            return
-
-        def run(offset, carry):
-            d = lax.rem(z * nx + x + offset, nz * nx)
-            step(d, {"vocab": lax.div(d, nx), "rows": lax.rem(d, nx)})
-            return carry
-
-        lax.fori_loop(1, nz * nx, run, 0)
-
-    barrier = pltpu.get_barrier_semaphore()
-
-    def greet(at):
-        pl.semaphore_signal(barrier, inc=1, device_id=at, device_id_type=pl.DeviceIdType.MESH)
-
-    def greet_line(offset, carry):
-        greet({"vocab": lax.rem(z + offset, nz)})
-        return carry
-
-    lax.fori_loop(1, nz, greet_line, 0, unroll=nz <= 4)
-    for i in range(1, nx * nc):
-        greet({"rows": lax.rem(x + i // nc, nx), "teach": lax.rem(c + i % nc, nc)})
 
     first = c == 0
     piece = direct.shape[2]
@@ -263,7 +263,16 @@
             device_id={"teach": 1 - c}, device_id_type=pl.DeviceIdType.MESH,
         ))
         swaps[-1].start()
+    step = depth // 14 if depth % (14 * LANES) == 0 else LANES
+    steps = range(0, depth, step)
+    early = len(steps) // 5
+
+    def weight_grad(k):
+        wg[:, k:k + step] = dot(grad, h[:, k:k + step], (0, 0)).astype(jnp.bfloat16)
+
     for s in range(halves):
+        for k in steps[s * early:(s + 1) * early]:
+            weight_grad(k)
         swaps[s].wait_recv()
         both = part[s].reshape(chips, nc, PACK, LANES)
         own_part = jnp.where(first, both[:, 0], both[:, 1])
@@ -278,9 +287,8 @@
         grecv[s, place] = gsend[s, place]
 
     div[...] = column_to_row([keep * (all_cross / all_sum_t - lse_t + lse_s)], rows)
-    step = depth // 7 if depth % (7 * LANES) == 0 else LANES
-    for k in range(0, depth, step):
-        wg[:, k:k + step] = dot(grad, h[:, k:k + step], (0, 0)).astype(jnp.bfloat16)
+    for k in steps[2 * early:]:
+        weight_grad(k)
 
     for s in range(halves):
         rest = grecv.at[s, pl.ds(0, chips - 1)]

time: 21.8 us -> 21.9 us (level)
  no operation moved by 1% of the time
where the time goes in v8:
time: 21.9 us; the launch traced here: 21.7 us
  Pallas kernels  21.1 us (96%)
  between operations  0.64 us (3%)
    pallas_call x1, Pallas kernels, body(): pl.pallas_call(functools.partial(main_kernel, sizes), out_shape=results,...  19.7 us
    pallas_call x1, Pallas kernels, body(): pl.pallas_call(write_kernel, out_shape=results, in_specs=[vmem, vmem, vme...  1.4 us

profile of v8, /device:TPU:0, one launch (start us, length us, event | category | flops | bytes accessed | tf_op | source)
XLA Modules:
  0.0 21.7 jit_solution(631741688804405079)
XLA Ops:
  0.6 19.7 %shard_map.67 = (bf16[304,3584]{1,0:T(8,128)(2,1)S(1)}, bf16[1,3584]{1,0:T(2,128)(2,1)S(1)}, f32[1,16]{1,0:T(1,128)S(1)}) custom-call(bf16[4,3584]{1,0:T(4,128)(2,1)} %hid_hbm.1, f32[8,608]{1,0:T(8,128)} %mentor_hbm.1, bf16[304,3584]{1,0:T(8,128)(2,1)} %w_hbm.1, s32[1,16]{1,0:T(1,128)} %bitcast.2), custom_call_target="tpu_custom_call" | custom-call | tf_op jit(solution)/shard_map/pallas_call | solution.py:348
  20.3 1.4 %shard_map.68 = (bf16[304,3584]{1,0:T(8,128)(2,1)}, bf16[1,3584]{1,0:T(2,128)(2,1)}, f32[1,16]{1,0:T(1,128)}) custom-call(bf16[304,3584]{1,0:T(8,128)(2,1)S(1)} %get-tuple-element.9.wg, bf16[1,3584]{1,0:T(2,128)(2,1)S(1)} %get-tuple-element.10.hg, f32[1,16]{1,0:T(1,128)S(1)} %get-tuple-element.11.div), custom_call_target="tpu_custom_call" | custom-call | tf_op jit(solution)/shard_map/pallas_call | solution.py:378

commit v9 on v8

--- a/solution.py
+++ b/solution.py
@@ -46,6 +46,16 @@
                 value = value + (1 - 2 * lax.rem(lax.div(index, 1 << bit), 2)) * (1 << bit)
         result.append(value)
     return result
+
+
+def flipped(index, k, size):
+    if size & (size - 1):
+        return lax.rem(index + k, size)
+    value = index
+    for bit in range(size.bit_length() - 1):
+        has, flip = (lax.rem(lax.div(v, 1 << bit), 2) for v in (index, k))
+        value = value + flip * (1 - 2 * has) * (1 << bit)
+    return value
 
 
 def main_kernel(
@@ -71,36 +81,22 @@
     me = (z * nx + x) * nc + c
 
     def others(step):
-        if unrolled:
-            zs, xs, cs = partners(z, nz), partners(x, nx), partners(c, nc)
-            for i in reversed(range(1, n)):
-                zz, xx, cc = zs[i // (nx * nc)], xs[i // nc % nx], cs[i % nc]
-                step((zz * nx + xx) * nc + cc, {"vocab": zz, "rows": xx, "teach": cc})
-            return
-
-        def run(offset, carry):
-            d = lax.rem(me + offset, n)
+        def run(i, carry):
+            d = flipped(me, n - 1 - i, n)
             step(d, {
                 "vocab": lax.div(d, nx * nc), "rows": lax.rem(lax.div(d, nc), nx), "teach": lax.rem(d, nc),
             })
             return carry
 
-        lax.fori_loop(1, n, run, 0)
+        lax.fori_loop(0, n - 1, run, 0)
 
     def same_core(step):
-        if unrolled:
-            zs, xs = partners(z, nz), partners(x, nx)
-            for i in reversed(range(1, nz * nx)):
-                zz, xx = zs[i // nx], xs[i % nx]
-                step(zz * nx + xx, {"vocab": zz, "rows": xx})
-            return
-
-        def run(offset, carry):
-            d = lax.rem(z * nx + x + offset, nz * nx)
+        def run(i, carry):
+            d = flipped(z * nx + x, nz * nx - 1 - i, nz * nx)
             step(d, {"vocab": lax.div(d, nx), "rows": lax.rem(d, nx)})
             return carry
 
-        lax.fori_loop(1, nz * nx, run, 0)
+        lax.fori_loop(0, nz * nx - 1, run, 0)
 
     barrier = pltpu.get_barrier_semaphore()
 
@@ -264,15 +260,17 @@
         ))
         swaps[-1].start()
     step = depth // 14 if depth % (14 * LANES) == 0 else LANES
-    steps = range(0, depth, step)
-    early = len(steps) // 5
-
-    def weight_grad(k):
-        wg[:, k:k + step] = dot(grad, h[:, k:k + step], (0, 0)).astype(jnp.bfloat16)
+    early = depth // step // 5
+
+    grad_t = grad.astype(jnp.float32).T.astype(jnp.bfloat16)
+
+    def weight_grad(i, carry):
+        at = pl.ds(pl.multiple_of(i * step, step), step)
+        wg[:, at] = dot(grad_t, h[:, at], (1, 0)).astype(jnp.bfloat16)
+        return carry
 
     for s in range(halves):
-        for k in steps[s * early:(s + 1) * early]:
-            weight_grad(k)
+        lax.fori_loop(s * early, (s + 1) * early, weight_grad, 0)
         swaps[s].wait_recv()
         both = part[s].reshape(chips, nc, PACK, LANES)
         own_part = jnp.where(first, both[:, 0], both[:, 1])
@@ -287,8 +285,7 @@
         grecv[s, place] = gsend[s, place]
 
     div[...] = column_to_row([keep * (all_cross / all_sum_t - lse_t + lse_s)], rows)
-    for k in steps[2 * early:]:
-        weight_grad(k)
+    lax.fori_loop(halves * early, depth // step, weight_grad, 0)
 
     for s in range(halves):
         rest = grecv.at[s, pl.ds(0, chips - 1)]

time: 21.9 us -> 22 us (level)
  no operation moved by 1% of the time
where the time goes in v9:
time: 22 us; the launch traced here: 21.8 us
  Pallas kernels  21.2 us (96%)
  between operations  0.64 us (3%)
    pallas_call x1, Pallas kernels, body(): pl.pallas_call(functools.partial(main_kernel, sizes), out_shape=results,...  19.8 us
    pallas_call x1, Pallas kernels, body(): pl.pallas_call(write_kernel, out_shape=results, in_specs=[vmem, vmem, vme...  1.4 us

profile of v9, /device:TPU:0, one launch (start us, length us, event | category | flops | bytes accessed | tf_op | source)
XLA Modules:
  0.0 21.8 jit_solution(4932368736332239157)
XLA Ops:
  0.6 19.8 %shard_map.67 = (bf16[304,3584]{1,0:T(8,128)(2,1)S(1)}, bf16[1,3584]{1,0:T(2,128)(2,1)S(1)}, f32[1,16]{1,0:T(1,128)S(1)}) custom-call(bf16[4,3584]{1,0:T(4,128)(2,1)} %hid_hbm.1, f32[8,608]{1,0:T(8,128)} %mentor_hbm.1, bf16[304,3584]{1,0:T(8,128)(2,1)} %w_hbm.1, s32[1,16]{1,0:T(1,128)} %bitcast.2), custom_call_target="tpu_custom_call" | custom-call | tf_op jit(solution)/shard_map/pallas_call | solution.py:345
  20.4 1.4 %shard_map.68 = (bf16[304,3584]{1,0:T(8,128)(2,1)}, bf16[1,3584]{1,0:T(2,128)(2,1)}, f32[1,16]{1,0:T(1,128)}) custom-call(bf16[304,3584]{1,0:T(8,128)(2,1)S(1)} %get-tuple-element.9.wg, bf16[1,3584]{1,0:T(2,128)(2,1)S(1)} %get-tuple-element.10.hg, f32[1,16]{1,0:T(1,128)S(1)} %get-tuple-element.11.div), custom_call_target="tpu_custom_call" | custom-call | tf_op jit(solution)/shard_map/pallas_call | solution.py:375

commit v10 on v9

--- a/solution.py
+++ b/solution.py
@@ -62,9 +62,9 @@
     sizes,
     hid_hbm, mentor_hbm, w_hbm, mask_hbm,
     wg, hg, div,
-    hid, mentor, mask, w, hsend, direct, relayed, h, tsend, trecv, ssend, srecv, part, theirs_part, gsend, grecv,
+    hid, mentor, mask, w, direct, relayed, h, tsend, trecv, ssend, srecv, part, theirs_part, gsend, grecv,
     hid_sem, mentor_sem, mask_sem, w_sem,
-    hs_sem, rs_sem, rr_sem, ts_sem, tr_sem, ss_sem, sr_sem, hr_sem, ps_sem, pr_sem, gs_sem, gr_sem,
+    rs_sem, rr_sem, ts_sem, tr_sem, ss_sem, sr_sem, hr_sem, up_sem, down_sem, ps_sem, pr_sem, gs_sem, gr_sem,
 ):
     nz, nx, nc = sizes
     n = nz * nx * nc
@@ -103,11 +103,9 @@
     def greet(at):
         pl.semaphore_signal(barrier, inc=1, device_id=at, device_id_type=pl.DeviceIdType.MESH)
 
-    def greet_line(offset, carry):
-        greet({"vocab": lax.rem(z + offset, nz)})
-        return carry
-
-    lax.fori_loop(1, nz, greet_line, 0, unroll=nz <= 4)
+    has_up, has_down = z < nz - 1, z > 0
+    pl.when(has_up)(lambda: greet({"vocab": z + 1}))
+    pl.when(has_down)(lambda: greet({"vocab": z - 1}))
     for i in range(1, nx * nc):
         greet({"rows": lax.rem(x + i // nc, nx), "teach": lax.rem(c + i % nc, nc)})
 
@@ -127,39 +125,29 @@
     hidden = hid[...].astype(jnp.float32)
     packed = jnp.concatenate([hidden[:, k * span:(k + 1) * span] for k in range(fold)], axis=0).astype(jnp.bfloat16)
     low, high = packed[:, :piece], packed[:, rest_of:]
-    hsend[...] = jnp.where(first, low, high)
     direct[z] = jnp.where(first, low, high)
     relayed[z] = jnp.where(first, high, low)
 
-    pl.semaphore_wait(barrier, nz - 1 + nx * nc - 1)
-
-    def send_hidden(to):
-        pltpu.make_async_remote_copy(
-            src_ref=hsend, dst_ref=direct.at[z], send_sem=hs_sem, recv_sem=hr_sem.at[z],
-            device_id={"vocab": to}, device_id_type=pl.DeviceIdType.MESH,
-        ).start()
-
-    def relay(source):
-        pltpu.make_async_copy(hsend, direct.at[source], hr_sem.at[source]).wait()
+    neighbours = jnp.where(has_up, 1, 0) + jnp.where(has_down, 1, 0)
+    pl.semaphore_wait(barrier, neighbours + nx * nc - 1)
+
+    def hop(source, up):
+        return pltpu.make_async_remote_copy(
+            src_ref=direct.at[source], dst_ref=direct.at[source],
+            send_sem=(up_sem if up else down_sem).at[source], recv_sem=hr_sem.at[source],
+            device_id={"vocab": z + 1 if up else z - 1}, device_id_type=pl.DeviceIdType.MESH,
+        )
+
+    pl.when(has_up)(lambda: hop(z, True).start())
+    pl.when(has_down)(lambda: hop(z, False).start())
+
+    def receive(source, up):
+        pltpu.make_async_copy(direct.at[source], direct.at[source], hr_sem.at[source]).wait()
+        pl.when(has_up if up else has_down)(lambda: hop(source, up).start())
         pltpu.make_async_remote_copy(
             src_ref=direct.at[source], dst_ref=relayed.at[source], send_sem=rs_sem, recv_sem=rr_sem,
             device_id={"teach": 1 - c}, device_id_type=pl.DeviceIdType.MESH,
         ).start()
-
-    def line(step, far_first):
-        if unrolled:
-            peers = partners(z, nz)[1:]
-            for zz in reversed(peers) if far_first else peers:
-                step(zz)
-            return
-
-        def run(offset, carry):
-            step(lax.rem(z + offset, nz))
-            return carry
-
-        lax.fori_loop(1, nz, run, 0)
-
-    line(send_hidden, True)
 
     inputs[1].wait()
     low = mentor[:, :vocab]
@@ -175,7 +163,10 @@
     inputs[2].wait()
     keep = row_to_column(mask[...].astype(jnp.float32), 0, rows)
 
-    line(relay, False)
+    for k in range(1, nz):
+        pl.when(z - k >= 0)(lambda k=k: receive(z - k, True))
+    for k in range(1, nz):
+        pl.when(z + k < nz)(lambda k=k: receive(z + k, False))
 
     teacher_copy.wait_recv()
     theirs = trecv[:, :vocab]
@@ -295,7 +286,9 @@
             at = s * reach + k * LANES
             hg[:, at:at + LANES] = total[k:k + 1].astype(jnp.bfloat16)
 
-    pltpu.make_async_copy(peers, peers, hs_sem).wait()
+    for k in range(nz):
+        pl.when(jnp.logical_and(has_up, k <= z))(lambda k=k: hop(k, True).wait_send())
+        pl.when(jnp.logical_and(has_down, k >= z))(lambda k=k: hop(k, False).wait_send())
     pltpu.make_async_copy(peers, peers, rs_sem).wait()
     teacher_copy.wait_send()
     for swap in swaps:
@@ -352,7 +345,6 @@
             pltpu.VMEM(mentor_unnormalized.shape, jnp.float32),
             pltpu.VMEM((1, rows), jnp.int32),
             pltpu.VMEM((vocab, depth), jnp.bfloat16),
-            pltpu.VMEM((PACK, piece), jnp.bfloat16),
             pltpu.VMEM((nz, PACK, piece), jnp.bfloat16),
             pltpu.VMEM((nz, PACK, piece), jnp.bfloat16),
             pltpu.VMEM((rows, depth), jnp.bfloat16),
@@ -364,7 +356,7 @@
             pltpu.VMEM((halves, rows // nc, PACK, LANES), jnp.float32),
             pltpu.VMEM((halves, rows // nc, PACK, LANES), jnp.bfloat16),
             pltpu.VMEM((halves, rows // nc, PACK, LANES), jnp.bfloat16),
-        ] + [dma] * 11 + [dma((nz,))] + [dma((halves,))] * 4,
+        ] + [dma] * 10 + [dma((nz,))] * 3 + [dma((halves,))] * 4,
         compiler_params=pltpu.CompilerParams(
             collective_id=0, has_side_effects=True, vmem_limit_bytes=44 * 2**20
         ),

time: 22 us -> 27.8 us (1.26)
  Pallas kernels: 21.2 us -> 27 us
    pallas_call x1, Pallas kernels: 19.8 us -> 25.6 us  [body(): pl.pallas_call(functools.partial(main_kernel, sizes), out_shape=results,...]
where the time goes in v10:
time: 27.8 us; the launch traced here: 27.6 us
  Pallas kernels  27 us (97%)
  between operations  0.64 us (2%)
    pallas_call x1, Pallas kernels, body(): pl.pallas_call(functools.partial(main_kernel, sizes), out_shape=results,...  25.6 us
    pallas_call x1, Pallas kernels, body(): pl.pallas_call(write_kernel, out_shape=results, in_specs=[vmem, vmem, vme...  1.4 us

profile of v10, /device:TPU:0, one launch (start us, length us, event | category | flops | bytes accessed | tf_op | source)
XLA Modules:
  0.0 27.6 jit_solution(11266966099508912017)
XLA Ops:
  0.6 25.6 %shard_map.67 = (bf16[304,3584]{1,0:T(8,128)(2,1)S(1)}, bf16[1,3584]{1,0:T(2,128)(2,1)S(1)}, f32[1,16]{1,0:T(1,128)S(1)}) custom-call(bf16[4,3584]{1,0:T(4,128)(2,1)} %hid_hbm.1, f32[8,608]{1,0:T(8,128)} %mentor_hbm.1, bf16[304,3584]{1,0:T(8,128)(2,1)} %w_hbm.1, s32[1,16]{1,0:T(1,128)} %bitcast.2), custom_call_target="tpu_custom_call" | custom-call | tf_op jit(solution)/shard_map/pallas_call | solution.py:338
  26.2 1.4 %shard_map.68 = (bf16[304,3584]{1,0:T(8,128)(2,1)}, bf16[1,3584]{1,0:T(2,128)(2,1)}, f32[1,16]{1,0:T(1,128)}) custom-call(bf16[304,3584]{1,0:T(8,128)(2,1)S(1)} %get-tuple-element.9.wg, bf16[1,3584]{1,0:T(2,128)(2,1)S(1)} %get-tuple-element.10.hg, f32[1,16]{1,0:T(1,128)S(1)} %get-tuple-element.11.div), custom_call_target="tpu_custom_call" | custom-call | tf_op jit(solution)/shard_map/pallas_call | solution.py:367

commit v11 on v8

--- a/solution.py
+++ b/solution.py
@@ -52,9 +52,9 @@
     sizes,
     hid_hbm, mentor_hbm, w_hbm, mask_hbm,
     wg, hg, div,
-    hid, mentor, mask, w, hsend, direct, relayed, h, tsend, trecv, ssend, srecv, part, theirs_part, gsend, grecv,
+    hid, mentor, mask, w, hsend, direct, h, tsend, trecv, ssend, srecv, part, theirs_part, gsend, grecv,
     hid_sem, mentor_sem, mask_sem, w_sem,
-    hs_sem, rs_sem, rr_sem, ts_sem, tr_sem, ss_sem, sr_sem, hr_sem, ps_sem, pr_sem, gs_sem, gr_sem,
+    hs_sem, ts_sem, tr_sem, ss_sem, sr_sem, hr_sem, ps_sem, pr_sem, gs_sem, gr_sem,
 ):
     nz, nx, nc = sizes
     n = nz * nx * nc
@@ -126,14 +126,11 @@
 
     first = c == 0
     piece = direct.shape[2]
-    rest_of = span - piece
     inputs[0].wait()
     hidden = hid[...].astype(jnp.float32)
     packed = jnp.concatenate([hidden[:, k * span:(k + 1) * span] for k in range(fold)], axis=0).astype(jnp.bfloat16)
-    low, high = packed[:, :piece], packed[:, rest_of:]
-    hsend[...] = jnp.where(first, low, high)
-    direct[z] = jnp.where(first, low, high)
-    relayed[z] = jnp.where(first, high, low)
+    hsend[...] = packed
+    direct[z] = packed
 
     pl.semaphore_wait(barrier, nz - 1 + nx * nc - 1)
 
@@ -145,10 +142,6 @@
 
     def relay(source):
         pltpu.make_async_copy(hsend, direct.at[source], hr_sem.at[source]).wait()
-        pltpu.make_async_remote_copy(
-            src_ref=direct.at[source], dst_ref=relayed.at[source], send_sem=rs_sem, recv_sem=rr_sem,
-            device_id={"teach": 1 - c}, device_id_type=pl.DeviceIdType.MESH,
-        ).start()
 
     def line(step, far_first):
         if unrolled:
@@ -199,15 +192,9 @@
 
     logits = jnp.zeros((rows, vocab), jnp.float32)
     for k in range(fold):
-        at = pl.multiple_of(k * span + c * rest_of, LANES)
+        at = pl.multiple_of(k * span, LANES)
         logits += dot(columns_of(direct, k, 0, piece), w[:, pl.ds(at, piece)], (1, 1))
-    peers = relayed.at[pl.ds(0, nz - 1)]
-    pltpu.make_async_copy(peers, peers, rr_sem).wait()
-    for k in range(fold):
-        start = pl.multiple_of((1 - c) * (piece - rest_of), LANES)
-        at = pl.multiple_of(k * span + (1 - c) * piece, LANES)
-        logits += dot(columns_of(relayed, k, start, rest_of), w[:, pl.ds(at, rest_of)], (1, 1))
-
+    peers = direct.at[pl.ds(0, nz - 1)]
     student = logits * (1.0 / smoothing_divisor)
     max_s = jnp.max(student, axis=1, keepdims=True)
     weight_s = jnp.exp(student - max_s)
@@ -226,9 +213,7 @@
     )
     arrived = []
     for k in range(nz):
-        low = jnp.where(first, direct[k], relayed[k])
-        high = jnp.where(first, relayed[k], direct[k])
-        arrived.append(jnp.concatenate([low, high[:, piece - rest_of:]], axis=1).astype(jnp.float32))
+        arrived.append(direct[k].astype(jnp.float32))
     for k in range(fold):
         h[:, k * span:(k + 1) * span] = jnp.concatenate(
             [a[k * own:(k + 1) * own] for a in arrived], axis=0
@@ -299,7 +284,6 @@
             hg[:, at:at + LANES] = total[k:k + 1].astype(jnp.bfloat16)
 
     pltpu.make_async_copy(peers, peers, hs_sem).wait()
-    pltpu.make_async_copy(peers, peers, rs_sem).wait()
     teacher_copy.wait_send()
     for swap in swaps:
         swap.wait_send()
@@ -332,7 +316,7 @@
     assert rows == n and nc == 2 and PACK % own == 0
     fold = PACK // own
     assert depth % (fold * LANES) == 0
-    piece = -(-depth // (fold * nc * LANES)) * LANES
+    piece = depth // fold
     halves = 2
     assert depth % (halves * LANES) == 0 and depth // (halves * LANES) <= PACK
     wide = -(-vocab // LANES) * LANES
@@ -357,7 +341,6 @@
             pltpu.VMEM((vocab, depth), jnp.bfloat16),
             pltpu.VMEM((PACK, piece), jnp.bfloat16),
             pltpu.VMEM((nz, PACK, piece), jnp.bfloat16),
-            pltpu.VMEM((nz, PACK, piece), jnp.bfloat16),
             pltpu.VMEM((rows, depth), jnp.bfloat16),
             pltpu.VMEM((half, wide), jnp.float32),
             pltpu.VMEM((half, wide), jnp.float32),
@@ -367,7 +350,7 @@
             pltpu.VMEM((halves, rows // nc, PACK, LANES), jnp.float32),
             pltpu.VMEM((halves, rows // nc, PACK, LANES), jnp.bfloat16),
             pltpu.VMEM((halves, rows // nc, PACK, LANES), jnp.bfloat16),
-        ] + [dma] * 11 + [dma((nz,))] + [dma((halves,))] * 4,
+        ] + [dma] * 9 + [dma((nz,))] + [dma((halves,))] * 4,
         compiler_params=pltpu.CompilerParams(
             collective_id=0, has_side_effects=True, vmem_limit_bytes=44 * 2**20
         ),

time: 21.9 us -> 22.3 us (1.018)
  Pallas kernels: 21.1 us -> 21.5 us
    pallas_call x1, Pallas kernels: 19.7 us -> 20.1 us  [body(): pl.pallas_call(functools.partial(main_kernel, sizes), out_shape=results,...]
where the time goes in v11:
time: 22.3 us; the launch traced here: 22.2 us
  Pallas kernels  21.5 us (96%)
  between operations  0.64 us (3%)
    pallas_call x1, Pallas kernels, body(): pl.pallas_call(functools.partial(main_kernel, sizes), out_shape=results,...  20.1 us
    pallas_call x1, Pallas kernels, body(): pl.pallas_call(write_kernel, out_shape=results, in_specs=[vmem, vmem, vme...  1.4 us

profile of v11, /device:TPU:0, one launch (start us, length us, event | category | flops | bytes accessed | tf_op | source)
XLA Modules:
  0.0 22.2 jit_solution(12869333976447219692)
XLA Ops:
  0.6 20.1 %shard_map.67 = (bf16[304,3584]{1,0:T(8,128)(2,1)S(1)}, bf16[1,3584]{1,0:T(2,128)(2,1)S(1)}, f32[1,16]{1,0:T(1,128)S(1)}) custom-call(bf16[4,3584]{1,0:T(4,128)(2,1)} %hid_hbm.1, f32[8,608]{1,0:T(8,128)} %mentor_hbm.1, bf16[304,3584]{1,0:T(8,128)(2,1)} %w_hbm.1, s32[1,16]{1,0:T(1,128)} %bitcast.2), custom_call_target="tpu_custom_call" | custom-call | tf_op jit(solution)/shard_map/pallas_call | solution.py:332
  20.8 1.4 %shard_map.68 = (bf16[304,3584]{1,0:T(8,128)(2,1)}, bf16[1,3584]{1,0:T(2,128)(2,1)}, f32[1,16]{1,0:T(1,128)}) custom-call(bf16[304,3584]{1,0:T(8,128)(2,1)S(1)} %get-tuple-element.9.wg, bf16[1,3584]{1,0:T(2,128)(2,1)S(1)} %get-tuple-element.10.hg, f32[1,16]{1,0:T(1,128)S(1)} %get-tuple-element.11.div), custom_call_target="tpu_custom_call" | custom-call | tf_op jit(solution)/shard_map/pallas_call | solution.py:361
